TPU v7x, 512 devices: a whole 4x8x8 slice. The times are simulated.
512 devices in a mesh: shot: 64 (over x, z_lo, y), box: 8 (over z_hi, core).
Axes of the slice: x: 4, y: 8, z: 8 (z_hi: 4, z_lo: 2; z = z_hi * 2 + z_lo), core: 2. Of those that a mesh axis runs over, the one named last changes fastest.
Arguments:
- wave_prev: float32 [64, 64, 128, 128], P('shot', None, 'box'), may hold values from -6 to 6
- wave_now: float32 [64, 64, 128, 128], P('shot', None, 'box'), may hold values from -6 to 6
- adjoint_prev: float32 [64, 64, 128, 128], P('shot', None, 'box'), may hold values from -6 to 6
- adjoint_now: float32 [64, 64, 128, 128], P('shot', None, 'box'), may hold values from -6 to 6
- velocity: float32 [64, 128, 128], P(None, 'box'), may hold values from 0.2 to 0.42
- source_cell: int32 [64], P('shot'), may hold values from 0 to 1048575
- wavelet: float32 [64, 5], P('shot'), may hold values from -40 to 40
- receiver_cell: int32 [64, 128], P('shot'), may hold values from 2 to 1048450, as said below
- residual: float32 [64, 3, 128], P('shot'), may hold values from -40 to 40
Outputs:
- wave_out: float32 [64, 64, 128, 128], P('shot', None, 'box')
- adjoint_out: float32 [64, 64, 128, 128], P('shot', None, 'box')
- speed_out: float32 [64, 128, 128], P(None, 'box')
Inputs may be any that keep to these rules, and one draw needn't show every extreme that they name: `receiver_cell`: each shot's 128 receiver cells are distinct and lie in the plane at depth 2; an index is (x * 128 + y) * 128 + z.
All inputs are finite; a program needn't handle non-finite values.
Results may differ from a plain program's by a relative error of at most 0.00002.
Values sent between devices are 32-bit elements; how exact they have to be, the bound alone decides.
A program may use at most 64 MiB of HBM per device.

v0:
```python
import jax
import jax.numpy as jnp
from jax import lax
from jax.sharding import PartitionSpec as P

STEPS = 3
FINAL = 2
PASSES = 4


stencil_weights = (-205.0 / 72.0, 8.0 / 5.0, -1.0 / 5.0, 8.0 / 315.0, -1.0 / 560.0)
conduct_scale = 1.0
diffuse_rate = 0.1
step_length = 0.1
speed_floor = 0.16
speed_ceiling = 0.44


def with_halo(block, sides, width):
    for axis, dim in sides:
        count = lax.axis_size(axis)
        forward = [(i, i + 1) for i in range(count - 1)]
        backward = [(target, source) for source, target in forward]
        low = lax.ppermute(
            lax.slice_in_dim(block, block.shape[dim] - width, None, axis=dim), axis, forward
        )
        high = lax.ppermute(lax.slice_in_dim(block, 0, width, axis=dim), axis, backward)
        block = jnp.concatenate([low, block, high], axis=dim)
    return block


def in_blocks(value, dim, devices):
    before, after = (value.shape[:dim], value.shape[dim + 1 :])
    return jnp.moveaxis(value.reshape(*before, devices, -1, *after), dim, 0)


def sent_and_summed(value, axis, dim):
    blocks = in_blocks(value, dim, lax.axis_size(axis))
    arrived = lax.all_to_all(blocks, axis, split_axis=0, concat_axis=0, tiled=True)
    return arrived.sum(axis=0)


def side_by_side(arrays, axis, dim, along):
    ends, at = ([], 0)
    for a in arrays[:-1]:
        at += a.shape[along]
        ends.append(at)
    both = jnp.concatenate(arrays, axis=along)
    return tuple(jnp.split(sent_and_summed(both, axis, dim), ends, axis=along))


def padded_2(value, sides, width):
    edges = {}
    for axis, dim in sides:
        devices, length = (lax.axis_size(axis), value.shape[dim])
        up = [(i, (i + 1) % devices) for i in range(devices - 1)]
        last = lax.slice_in_dim(value, length - width, length, axis=dim)
        initial = lax.slice_in_dim(value, 0, width, axis=dim)
        edges[dim] = (
            lax.ppermute(last, axis, up),
            lax.ppermute(initial, axis, [(b, a) for a, b in up]),
        )
    done = []
    for _, dim in sides:
        low, high = edges[dim]
        around = [(width, width) if d in done else (0, 0) for d in range(value.ndim)]
        value = jnp.concatenate([jnp.pad(low, around), value, jnp.pad(high, around)], axis=dim)
        done.append(dim)
    return value


def copy_for_each(value, axis):
    copies = jnp.broadcast_to(value, (lax.axis_size(axis), *value.shape))
    return lax.all_to_all(copies, axis, split_axis=0, concat_axis=0, tiled=True)


def laid_out(blocks, dim):
    blocks = jnp.moveaxis(blocks, 0, dim)
    shape = blocks.shape
    return blocks.reshape(*shape[:dim], shape[dim] * shape[dim + 1], *shape[dim + 2 :])


def collect(value, axis, dim):
    blocks = copy_for_each(value, axis)
    return laid_out(blocks, dim)


def laplace(padded):
    count_first = padded.shape[-3] - 8
    count_second = padded.shape[-2] - 8
    count_third = padded.shape[-1] - 8

    def window(shift_first, shift_second, shift_third):
        return padded[
            ...,
            4 + shift_first : 4 + shift_first + count_first,
            4 + shift_second : 4 + shift_second + count_second,
            4 + shift_third : 4 + shift_third + count_third,
        ]

    summed = 3.0 * stencil_weights[0] * window(0, 0, 0)
    for offset in range(1, 5):
        weight = stencil_weights[offset]
        summed = summed + weight * (window(offset, 0, 0) + window(-offset, 0, 0))
        summed = summed + weight * (window(0, offset, 0) + window(0, -offset, 0))
        summed = summed + weight * (window(0, 0, offset) + window(0, 0, -offset))
    return summed


def conduct(rise):
    return rise / (1.0 + (rise / conduct_scale) ** 2)


def diffuse(smooth_in, padded, start_first, total_first, start_second, total_second):
    count_first = smooth_in.shape[0]
    count_second = smooth_in.shape[1]
    rise_first = padded[1:, 1:-1, :] - padded[:-1, 1:-1, :]
    face_first = start_first - 1 + lax.broadcasted_iota(jnp.int32, (count_first + 1, 1, 1), 0)
    interior_first = (face_first >= 0) & (face_first + 1 < total_first)
    flux_first = jnp.where(interior_first, conduct(rise_first), 0.0)
    rise_second = padded[1:-1, 1:, :] - padded[1:-1, :-1, :]
    face_second = start_second - 1 + lax.broadcasted_iota(jnp.int32, (1, count_second + 1, 1), 1)
    interior_second = (face_second >= 0) & (face_second + 1 < total_second)
    flux_second = jnp.where(interior_second, conduct(rise_second), 0.0)
    flux_third = conduct(smooth_in[:, :, 1:] - smooth_in[:, :, :-1])
    zero_face = jnp.zeros((count_first, count_second, 1), jnp.float32)
    flux_third = jnp.concatenate([zero_face, flux_third, zero_face], 2)
    change = (
        flux_first[1:]
        - flux_first[:-1]
        + (flux_second[:, 1:] - flux_second[:, :-1])
        + (flux_third[:, :, 1:] - flux_third[:, :, :-1])
    )
    return smooth_in + diffuse_rate * change


def locate(flat_index, total_second, depth_cells, rows_local, start_second):
    first_index = flat_index // (total_second * depth_cells)
    second_index = flat_index // depth_cells % total_second - start_second
    third_index = flat_index % depth_cells
    inside = (second_index >= 0) & (second_index < rows_local)
    return (first_index, jnp.clip(second_index, 0, rows_local - 1), third_index, inside)


def local(
    wave_prev,
    wave_now,
    adjoint_prev,
    adjoint_now,
    velocity,
    source_cell,
    wavelet,
    receiver_cell,
    residual,
):
    rows_first = velocity.shape[0]
    rows_local = velocity.shape[1]
    depth_cells = velocity.shape[2]
    total_second = rows_local * lax.axis_size("box")
    start_second = lax.axis_index("box") * rows_local
    source_first, source_second, source_third, source_inside = locate(
        source_cell[0], total_second, depth_cells, rows_local, start_second
    )
    earlier = jnp.concatenate([wave_prev, adjoint_prev], 0)
    current = jnp.concatenate([wave_now, adjoint_now], 0)
    gradient_local = jnp.zeros(velocity.shape, jnp.float32)
    illumination_local = jnp.zeros(velocity.shape, jnp.float32)
    margin = 4 * STEPS
    stacked = jnp.concatenate([earlier, current, velocity[None]], 0)
    extended = with_halo(stacked, (("box", 2),), margin)
    ext_earlier = extended[0:2]
    ext_current = extended[2:4]
    ext_velocity = extended[4]
    ext_square = ext_velocity * ext_velocity
    for step_index in range(STEPS):
        keep = margin - 4 * (step_index + 1)
        width = rows_local + 2 * keep
        offset = margin - keep
        band_start = start_second - keep
        padded = jnp.pad(ext_current, ((0, 0), (4, 4), (0, 0), (4, 4)))
        square_part = ext_square[:, offset : offset + width, :]
        following = (
            2.0 * ext_current[:, :, 4 : 4 + width]
            - ext_earlier[:, :, 4 : 4 + width]
            + square_part * laplace(padded)
        )
        global_second = band_start + lax.broadcasted_iota(jnp.int32, (1, 1, width, 1), 2)
        valid = (global_second >= 0) & (global_second < total_second)
        following = jnp.where(valid, following, 0.0)
        band_source = locate(source_cell[0], total_second, depth_cells, width, band_start)
        band_receiver = locate(receiver_cell[0], total_second, depth_cells, width, band_start)
        following = following.at[0, band_source[0], band_source[1], band_source[2]].add(
            jnp.where(band_source[3], wavelet[0, step_index], 0.0)
        )
        following = following.at[1, band_receiver[0], band_receiver[1], band_receiver[2]].add(
            jnp.where(band_receiver[3], residual[0, step_index], 0.0)
        )
        now_centre = ext_current[:, :, keep + 4 : keep + 4 + rows_local]
        early_centre = ext_earlier[:, :, keep + 4 : keep + 4 + rows_local]
        next_centre = following[:, :, keep : keep + rows_local]
        second_diff = next_centre[0] - 2.0 * now_centre[0] + early_centre[0]
        gradient_local = gradient_local + now_centre[1] * second_diff
        illumination_local = illumination_local + now_centre[0] * now_centre[0]
        ext_earlier = ext_current[:, :, 4 : 4 + width]
        ext_current = following
    earlier = ext_earlier
    current = ext_current
    adjoint_out = current[1][None]
    gradient_piece, illumination_piece = side_by_side(
        (gradient_local, illumination_local), "shot", 0, 1
    )
    rows_piece = gradient_piece.shape[0]
    start_first = lax.axis_index("shot") * rows_piece
    smoothed = gradient_piece / jnp.sqrt(illumination_piece + 1.0)
    for smooth_pass in range(PASSES):
        padded = padded_2(smoothed, (("shot", 0), ("box", 1)), 1)
        smoothed = diffuse(smoothed, padded, start_first, rows_first, start_second, total_second)
    speed_piece = lax.dynamic_slice_in_dim(velocity, start_first, rows_piece, 0)
    updated = jnp.clip(speed_piece - step_length * smoothed, speed_floor, speed_ceiling)
    new_speed = collect(updated, "shot", 0)
    new_square = new_speed * new_speed
    wave_earlier = earlier[0]
    wave_current = current[0]
    for step_index in range(FINAL):
        padded = with_halo(wave_current, (("box", 1),), 4)
        padded = jnp.pad(padded, ((4, 4), (0, 0), (4, 4)))
        following = 2.0 * wave_current - wave_earlier + new_square * laplace(padded)
        following = following.at[source_first, source_second, source_third].add(
            jnp.where(source_inside, wavelet[0, STEPS + step_index], 0.0)
        )
        wave_earlier, wave_current = (wave_current, following)
    return (wave_current[None], adjoint_out, new_speed)


def solution(mesh):
    return jax.shard_map(
        local,
        mesh=mesh,
        in_specs=(
            P("shot", None, "box", None),
            P("shot", None, "box", None),
            P("shot", None, "box", None),
            P("shot", None, "box", None),
            P(None, "box", None),
            P("shot"),
            P("shot", None),
            P("shot", None),
            P("shot", None, None),
        ),
        out_specs=(
            P("shot", None, "box", None),
            P("shot", None, "box", None),
            P(None, "box", None),
        ),
        check_vma=False,
    )
```

profile of v0, /device:TPU:1, one launch (start us, length us, event | category | flops | bytes accessed | tf_op | source)
XLA Modules:
  0.0 326.8 jit_solution(4173287245627632529)
XLA Ops:
  5.5 8.8 %collective-permute-start.1 = (f32[5,64,12,128]{3,1,2,0:T(8,128)}, f32[5,64,12,128]{3,1,2,0:T(8,128)}, u32[]{:S(2)}, u32[]{:S(2)}) collective-permute-start(f32[5,64,12,128]{3,1,2,0:T(8,128)} %copy.13), channel_id=1, source_target_pairs={{1,0},{2,1},{3,2},{4,3},{5,4},{6,5},{7,6},{9,8},{10,9},{11,10},{12... | collective-permute-start | bytes 5898248 | tf_op jit(solution)/shard_map/ppermute | solution.py:27
  23.3 33.1 %collective-permute-done.1 = f32[5,64,12,128]{3,1,2,0:T(8,128)} collective-permute-done((f32[5,64,12,128]{3,1,2,0:T(8,128)}, f32[5,64,12,128]{3,1,2,0:T(8,128)}, u32[]{:S(2)}, u32[]{:S(2)}) %collective-permute-start.1) | collective-permute-done | bytes 1966112 | tf_op jit(solution)/shard_map/ppermute | solution.py:27
  56.4 4.2 %copy.15 = f32[5,64,12,128]{3,2,1,0:T(8,128)} copy(f32[5,64,12,128]{3,1,2,0:T(8,128)} %collective-permute-done.1) | data formatting | bytes 3932160 | tf_op jit(solution)/shard_map/ppermute | solution.py:27
  60.6 4.2 %copy.14 = f32[5,64,12,128]{3,2,1,0:T(8,128)} copy(f32[5,64,12,128]{3,1,2,0:T(8,128)} %collective-permute-done) | data formatting | bytes 3932160 | tf_op jit(solution)/shard_map/ppermute | solution.py:24
  64.8 3.3 pad_maximum_fusion
  71.4 7.9 %fusion.33 = f32[2,64,32,128]{3,2,1,0:T(8,128)S(1)} fusion(f32[5,64,40,128]{3,2,1,0:T(8,128)S(1)} %pad_maximum_fusion, f32[2,64,40,128]{3,2,1,0:T(8,128)S(1)} %slice.1068, f32[64,32,128]{2,1,0:T(8,128)S(1)} %slice.1067, pred[32]{0:T(512)(128)(4,1)S(1)} %compare_and_fusion.2), kind=kLoop, calls=%fused_computation.94 | loop fusion | flops 22020096 | bytes 26738720 | tf_op jit(solution)/shard_map/jit(_where)/select_n | solution.py:189
  82.2 9.8 %scatter_fusion = f32[2,64,32,128]{3,2,1,0:T(8,128)S(1)} fusion(f32[2,64,32,128]{3,2,1,0:T(8,128)S(1)} %scatter-add.36, s32[128]{0:T(128)S(1)} %get-tuple-element.90, f32[128]{0:T(128)S(1)} %get-tuple-element.88), kind=kCustom, calls=%fused_computation | custom fusion | flops 128 | bytes 3584 | tf_op jit(solution)/shard_map/scatter-add | solution.py:195
  92.1 7.3 %fusion.70 = f32[2,64,24,128]{3,2,1,0:T(8,128)} fusion(f32[5,64,40,128]{3,2,1,0:T(8,128)} %copy-done, f32[2,64,32,128]{3,2,1,0:T(8,128)S(1)} %scatter_fusion, f32[64,24,128]{2,1,0:T(8,128)S(1)} %slice-done, pred[24]{0:T(512)(128)(4,1)S(1)} %compare_and_fusion.3), kind=kLoop, calls=%fused_computation.140 | loop fusion | flops 16515072 | bytes 20185600 | tf_op jit(solution)/shard_map/jit(_where)/select_n | solution.py:189
  103.9 18.5 %scatter_fusion.1 = f32[2,64,24,128]{3,2,1,0:T(8,128)} fusion(f32[2,64,24,128]{3,2,1,0:T(8,128)} %scatter-add.48, s32[128]{0:T(128)S(1)} %get-tuple-element.89, f32[128]{0:T(128)S(1)} %get-tuple-element.87), kind=kCustom, calls=%fused_computation.1 | custom fusion | flops 128 | bytes 3584 | tf_op jit(solution)/shard_map/scatter-add | solution.py:195
  122.4 19.1 %fusion.105 = f32[2,64,16,128]{3,2,1,0:T(8,128)S(1)} fusion(f32[2,64,32,128]{3,2,1,0:T(8,128)S(1)} %scatter_fusion, f32[2,64,24,128]{3,2,1,0:T(8,128)} %scatter_fusion.1, f32[64,16,128]{2,1,0:T(8,128)} %slice.1090, pred[16]{0:T(512)(128)(4,1)S(1)} %compare_and_fusion.4), kind=kLoop, calls=%fused_computation.193 | loop fusion | flops 11010048 | bytes 13631504 | tf_op jit(solution)/shard_map/jit(_where)/select_n | solution.py:189
  144.2 9.8 %scatter_fusion.2 = f32[2,64,16,128]{3,2,1,0:T(8,128)S(1)} fusion(f32[2,64,16,128]{3,2,1,0:T(8,128)S(1)} %scatter-add.50, s32[128]{0:T(128)S(1)} %get-tuple-element.65, f32[128]{0:T(128)S(1)} %get-tuple-element.63), kind=kCustom, calls=%fused_computation.2 | custom fusion | flops 128 | bytes 3584 | tf_op jit(solution)/shard_map/scatter-add | solution.py:195
  157.4 10.4 %all-to-all-start = ((f32[64,1,32,128]{3,2,1,0:T(8,128)}), f32[64,1,32,128]{3,2,1,0:T(8,128)S(1)}, u32[]{:S(2)}, u32[]{:S(2)}) async-start(f32[64,1,32,128]{3,2,1,0:T(8,128)} %maximum_bitcast_fusion), calls=%async_computation | async-start | bytes 2097152 | tf_op jit(solution)/shard_map/all_to_all | solution.py:39
  167.8 17.8 %all-to-all-done = f32[64,1,32,128]{3,2,1,0:T(8,128)S(1)} async-done(((f32[64,1,32,128]{3,2,1,0:T(8,128)}), f32[64,1,32,128]{3,2,1,0:T(8,128)S(1)}, u32[]{:S(2)}, u32[]{:S(2)}) %all-to-all-start) | async-done | bytes 1048608 | tf_op jit(solution)/shard_map/all_to_all | solution.py:39
  187.0 4.4 %collective-permute-start.3 = (f32[1,16,128]{2,1,0:T(8,128)S(1)}, f32[1,16,128]{2,1,0:T(8,128)S(1)}, u32[]{:S(2)}, u32[]{:S(2)}) collective-permute-start(f32[1,16,128]{2,1,0:T(8,128)S(1)} %fusion.219), channel_id=1, source_target_pairs={{0,8},{8,16},{16,24},{24,32},{32,40},{40,48},{48,56},{56,64},{64,7... | collective-permute-start | bytes 24584 | tf_op jit(solution)/shard_map/ppermute | solution.py:60
  191.5 16.3 %collective-permute-start.5 = (f32[1,1,128]{2,1,0:T(1,128)S(1)}, f32[1,1,128]{2,1,0:T(1,128)S(1)}, u32[]{:S(2)}, u32[]{:S(2)}) collective-permute-start(f32[1,1,128]{2,1,0:T(1,128)S(1)} %get-tuple-element.86), channel_id=1, source_target_pairs={{0,1},{1,2},{2,3},{3,4},{4,5},{5,6},{6,7},{8,9},{9,10},{10,11},{11... | collective-permute-start | bytes 1544 | tf_op jit(solution)/shard_map/ppermute | solution.py:60
  209.8 3.7 %collective-permute-done.4 = f32[1,1,128]{2,1,0:T(1,128)S(1)} collective-permute-done((f32[1,1,128]{2,1,0:T(1,128)S(1)}, f32[1,1,128]{2,1,0:T(1,128)S(1)}, u32[]{:S(2)}, u32[]{:S(2)}) %collective-permute-start.4) | collective-permute-done | bytes 544 | tf_op jit(solution)/shard_map/ppermute | solution.py:61
  215.0 4.3 %collective-permute-start.7 = (f32[1,16,128]{2,1,0:T(8,128)S(1)}, f32[1,16,128]{2,1,0:T(8,128)S(1)}, u32[]{:S(2)}, u32[]{:S(2)}) collective-permute-start(f32[1,16,128]{2,1,0:T(8,128)S(1)} %fusion.217), channel_id=1, source_target_pairs={{0,8},{8,16},{16,24},{24,32},{32,40},{40,48},{48,56},{56,64},{64,7... | collective-permute-start | bytes 24584 | tf_op jit(solution)/shard_map/ppermute | solution.py:60
  219.3 4.5 %collective-permute-start.9 = (f32[1,1,128]{2,1,0:T(1,128)S(1)}, f32[1,1,128]{2,1,0:T(1,128)S(1)}, u32[]{:S(2)}, u32[]{:S(2)}) collective-permute-start(f32[1,1,128]{2,1,0:T(1,128)S(1)} %get-tuple-element.84), channel_id=1, source_target_pairs={{0,1},{1,2},{2,3},{3,4},{4,5},{5,6},{6,7},{8,9},{9,10},{10,11},{11... | collective-permute-start | bytes 1544 | tf_op jit(solution)/shard_map/ppermute | solution.py:60
  225.8 5.3 %collective-permute-done.8 = f32[1,1,128]{2,1,0:T(1,128)S(1)} collective-permute-done((f32[1,1,128]{2,1,0:T(1,128)S(1)}, f32[1,1,128]{2,1,0:T(1,128)S(1)}, u32[]{:S(2)}, u32[]{:S(2)}) %collective-permute-start.8) | collective-permute-done | bytes 544 | tf_op jit(solution)/shard_map/ppermute | solution.py:61
  232.5 4.0 %collective-permute-start.11 = (f32[1,16,128]{2,1,0:T(8,128)S(1)}, f32[1,16,128]{2,1,0:T(8,128)S(1)}, u32[]{:S(2)}, u32[]{:S(2)}) collective-permute-start(f32[1,16,128]{2,1,0:T(8,128)S(1)} %fusion.213), channel_id=1, source_target_pairs={{0,8},{8,16},{16,24},{24,32},{32,40},{40,48},{48,56},{56,64},{64,7... | collective-permute-start | bytes 24584 | tf_op jit(solution)/shard_map/ppermute | solution.py:60
  236.6 2.5 collective-permute-start.13
  241.2 4.9 %collective-permute-done.12 = f32[1,1,128]{2,1,0:T(1,128)S(1)} collective-permute-done((f32[1,1,128]{2,1,0:T(1,128)S(1)}, f32[1,1,128]{2,1,0:T(1,128)S(1)}, u32[]{:S(2)}, u32[]{:S(2)}) %collective-permute-start.12) | collective-permute-done | bytes 544 | tf_op jit(solution)/shard_map/ppermute | solution.py:61
  247.6 4.0 %collective-permute-start.15 = (f32[1,16,128]{2,1,0:T(8,128)S(1)}, f32[1,16,128]{2,1,0:T(8,128)S(1)}, u32[]{:S(2)}, u32[]{:S(2)}) collective-permute-start(f32[1,16,128]{2,1,0:T(8,128)S(1)} %fusion.209), channel_id=1, source_target_pairs={{0,8},{8,16},{16,24},{24,32},{32,40},{40,48},{48,56},{56,64},{64,7... | collective-permute-start | bytes 24584 | tf_op jit(solution)/shard_map/ppermute | solution.py:60
  251.7 2.5 collective-permute-start.17
  256.3 4.9 %collective-permute-done.16 = f32[1,1,128]{2,1,0:T(1,128)S(1)} collective-permute-done((f32[1,1,128]{2,1,0:T(1,128)S(1)}, f32[1,1,128]{2,1,0:T(1,128)S(1)}, u32[]{:S(2)}, u32[]{:S(2)}) %collective-permute-start.16) | collective-permute-done | bytes 544 | tf_op jit(solution)/shard_map/ppermute | solution.py:61
  262.9 16.7 %all-to-all-start.1 = ((f32[64,1,16,128]{3,2,1,0:T(8,128)}), f32[64,1,16,128]{3,2,1,0:T(8,128)S(1)}, u32[]{:S(2)}, u32[]{:S(2)}) async-start(f32[64,1,16,128]{3,2,1,0:T(8,128)} %broadcast_in_dim.155), calls=%async_computation.1 | async-start | bytes 1048576 | tf_op jit(solution)/shard_map/all_to_all | solution.py:74
  280.5 2.3 collective-permute-start.18
  286.3 6.7 %collective-permute-done.19 = f32[64,4,128]{2,1,0:T(4,128)} collective-permute-done((f32[64,4,128]{2,1,0:T(4,128)S(1)}, f32[64,4,128]{2,1,0:T(4,128)}, u32[]{:S(2)}, u32[]{:S(2)}) %collective-permute-start.19) | collective-permute-done | bytes 131104 | tf_op jit(solution)/shard_map/ppermute | solution.py:27
  295.2 5.9 %fusion.140 = f32[64,16,128]{2,1,0:T(8,128)S(1)} fusion(f32[64,16,128]{2,1,0:T(8,128)} %copy-done.4, f32[64,4,128]{2,1,0:T(4,128)S(1)} %collective-permute-done.18, f32[64,4,128]{2,1,0:T(4,128)} %collective-permute-done.19, f32[72,24,136]{2,1,0:T(8,128)S(1)} %select_maximum_fusion.2, f32[2,64,24,128]{3,2,1,0:T(8,128)} %scatter_fusion.1, ...), kind=kLoop, calls=%fused_computation.241 | loop fusion | flops 6553600 | bytes 10747904 | tf_op jit(solution)/shard_map/add | solution.py:227
  308.8 2.4 collective-permute-start.21
  311.9 7.1 %collective-permute-done.21 = f32[64,4,128]{2,1,0:T(4,128)S(1)} collective-permute-done((f32[64,4,128]{2,1,0:T(4,128)S(1)}, f32[64,4,128]{2,1,0:T(4,128)S(1)}, u32[]{:S(2)}, u32[]{:S(2)}) %collective-permute-start.21) | collective-permute-done | bytes 131104 | tf_op jit(solution)/shard_map/ppermute | solution.py:27
  320.8 2.5 fusion.115
  (127 shorter events, 53.0 us)
Async XLA Ops:
  5.5 50.9 %collective-permute-start.1 = (f32[5,64,12,128]{3,1,2,0:T(8,128)}, f32[5,64,12,128]{3,1,2,0:T(8,128)}, u32[]{:S(2)}, u32[]{:S(2)}) collective-permute-start(f32[5,64,12,128]{3,1,2,0:T(8,128)} %copy.13), channel_id=1, source_target_pairs={{1,0},{2,1},{3,2},{4,3},{5,4},{6,5},{7,6},{9,8},{10,9},{11,10},{12... | collective-permute-start | bytes 5898248 | tf_op jit(solution)/shard_map/ppermute | solution.py:27
  14.3 7.4 %copy-start.15 = (s32[4]{0:T(128)S(1)}, s32[4]{0:T(128)}, u32[]{:S(2)}) copy-start(s32[4]{0:T(128)} %constant.302.clone.1) | copy-start | bytes 52
  14.3 8.1 %copy-start.13 = (s32[4]{0:T(128)S(1)}, s32[4]{0:T(128)}, u32[]{:S(2)}) copy-start(s32[4]{0:T(128)} %constant.309.clone.1) | copy-start | bytes 52
  14.3 8.1 %copy-start.14 = (s32[4]{0:T(128)S(1)}, s32[4]{0:T(128)}, u32[]{:S(2)}) copy-start(s32[4]{0:T(128)} %constant.306.clone.1) | copy-start | bytes 52
  14.3 8.9 %copy-start.10 = (s32[1,128]{1,0:T(1,128)S(1)}, s32[1,128]{1,0:T(1,128)}, u32[]{:S(2)}) copy-start(s32[1,128]{1,0:T(1,128)} %param.26) | copy-start | bytes 1540
  14.3 8.9 %copy-start.11 = (f32[1,3,128]{2,0,1:T(1,128)S(1)}, f32[1,3,128]{2,0,1:T(1,128)}, u32[]{:S(2)}) copy-start(f32[1,3,128]{2,0,1:T(1,128)} %param.27) | copy-start | bytes 4612
  16.3 44.2 %collective-permute-start = (f32[5,64,12,128]{3,1,2,0:T(8,128)}, f32[5,64,12,128]{3,1,2,0:T(8,128)}, u32[]{:S(2)}, u32[]{:S(2)}) collective-permute-start(f32[5,64,12,128]{3,1,2,0:T(8,128)} %copy.12), channel_id=1, source_target_pairs={{0,1},{1,2},{2,3},{3,4},{4,5},{5,6},{6,7},{8,9},{9,10},{10,11},{11... | collective-permute-start | bytes 5898248 | tf_op jit(solution)/shard_map/ppermute | solution.py:24
  71.4 20.7 %slice-start = ((f32[64,40,128]{2,1,0:T(8,128)}), f32[64,24,128]{2,1,0:T(8,128)S(1)}, s32[]{:S(2)}) async-start(f32[64,40,128]{2,1,0:T(8,128)} %copy-done.1), calls=%async_computation.2 | async-start | bytes 1572864 | tf_op jit(solution)/shard_map/slice | solution.py:181
  157.4 28.2 %all-to-all-start = ((f32[64,1,32,128]{3,2,1,0:T(8,128)}), f32[64,1,32,128]{3,2,1,0:T(8,128)S(1)}, u32[]{:S(2)}, u32[]{:S(2)}) async-start(f32[64,1,32,128]{3,2,1,0:T(8,128)} %maximum_bitcast_fusion), calls=%async_computation | async-start | bytes 2097152 | tf_op jit(solution)/shard_map/all_to_all | solution.py:39
  185.7 24.0 %collective-permute-start.2 = (f32[1,16,128]{2,1,0:T(8,128)S(1)}, f32[1,16,128]{2,1,0:T(8,128)S(1)}, u32[]{:S(2)}, u32[]{:S(2)}) collective-permute-start(f32[1,16,128]{2,1,0:T(8,128)S(1)} %fusion.219), channel_id=1, source_target_pairs={{8,0},{16,8},{24,16},{32,24},{40,32},{48,40},{56,48},{64,56},{72,6... | collective-permute-start | bytes 24584 | tf_op jit(solution)/shard_map/ppermute | solution.py:61
  187.0 22.7 %collective-permute-start.3 = (f32[1,16,128]{2,1,0:T(8,128)S(1)}, f32[1,16,128]{2,1,0:T(8,128)S(1)}, u32[]{:S(2)}, u32[]{:S(2)}) collective-permute-start(f32[1,16,128]{2,1,0:T(8,128)S(1)} %fusion.219), channel_id=1, source_target_pairs={{0,8},{8,16},{16,24},{24,32},{32,40},{40,48},{48,56},{56,64},{64,7... | collective-permute-start | bytes 24584 | tf_op jit(solution)/shard_map/ppermute | solution.py:60
  191.5 18.3 %collective-permute-start.5 = (f32[1,1,128]{2,1,0:T(1,128)S(1)}, f32[1,1,128]{2,1,0:T(1,128)S(1)}, u32[]{:S(2)}, u32[]{:S(2)}) collective-permute-start(f32[1,1,128]{2,1,0:T(1,128)S(1)} %get-tuple-element.86), channel_id=1, source_target_pairs={{0,1},{1,2},{2,3},{3,4},{4,5},{5,6},{6,7},{8,9},{9,10},{10,11},{11... | collective-permute-start | bytes 1544 | tf_op jit(solution)/shard_map/ppermute | solution.py:60
  207.8 5.8 %collective-permute-start.4 = (f32[1,1,128]{2,1,0:T(1,128)S(1)}, f32[1,1,128]{2,1,0:T(1,128)S(1)}, u32[]{:S(2)}, u32[]{:S(2)}) collective-permute-start(f32[1,1,128]{2,1,0:T(1,128)S(1)} %get-tuple-element.85), channel_id=1, source_target_pairs={{1,0},{2,1},{3,2},{4,3},{5,4},{6,5},{7,6},{9,8},{10,9},{11,10},{12... | collective-permute-start | bytes 1544 | tf_op jit(solution)/shard_map/ppermute | solution.py:61
  213.7 12.1 %collective-permute-start.6 = (f32[1,16,128]{2,1,0:T(8,128)S(1)}, f32[1,16,128]{2,1,0:T(8,128)S(1)}, u32[]{:S(2)}, u32[]{:S(2)}) collective-permute-start(f32[1,16,128]{2,1,0:T(8,128)S(1)} %fusion.217), channel_id=1, source_target_pairs={{8,0},{16,8},{24,16},{32,24},{40,32},{48,40},{56,48},{64,56},{72,6... | collective-permute-start | bytes 24584 | tf_op jit(solution)/shard_map/ppermute | solution.py:61
  215.0 10.8 %collective-permute-start.7 = (f32[1,16,128]{2,1,0:T(8,128)S(1)}, f32[1,16,128]{2,1,0:T(8,128)S(1)}, u32[]{:S(2)}, u32[]{:S(2)}) collective-permute-start(f32[1,16,128]{2,1,0:T(8,128)S(1)} %fusion.217), channel_id=1, source_target_pairs={{0,8},{8,16},{16,24},{24,32},{32,40},{40,48},{48,56},{56,64},{64,7... | collective-permute-start | bytes 24584 | tf_op jit(solution)/shard_map/ppermute | solution.py:60
  219.3 6.5 %collective-permute-start.9 = (f32[1,1,128]{2,1,0:T(1,128)S(1)}, f32[1,1,128]{2,1,0:T(1,128)S(1)}, u32[]{:S(2)}, u32[]{:S(2)}) collective-permute-start(f32[1,1,128]{2,1,0:T(1,128)S(1)} %get-tuple-element.84), channel_id=1, source_target_pairs={{0,1},{1,2},{2,3},{3,4},{4,5},{5,6},{6,7},{8,9},{9,10},{10,11},{11... | collective-permute-start | bytes 1544 | tf_op jit(solution)/shard_map/ppermute | solution.py:60
  223.8 7.3 %collective-permute-start.8 = (f32[1,1,128]{2,1,0:T(1,128)S(1)}, f32[1,1,128]{2,1,0:T(1,128)S(1)}, u32[]{:S(2)}, u32[]{:S(2)}) collective-permute-start(f32[1,1,128]{2,1,0:T(1,128)S(1)} %get-tuple-element.83), channel_id=1, source_target_pairs={{1,0},{2,1},{3,2},{4,3},{5,4},{6,5},{7,6},{9,8},{10,9},{11,10},{12... | collective-permute-start | bytes 1544 | tf_op jit(solution)/shard_map/ppermute | solution.py:61
  231.3 9.9 %collective-permute-start.10 = (f32[1,16,128]{2,1,0:T(8,128)S(1)}, f32[1,16,128]{2,1,0:T(8,128)S(1)}, u32[]{:S(2)}, u32[]{:S(2)}) collective-permute-start(f32[1,16,128]{2,1,0:T(8,128)S(1)} %fusion.213), channel_id=1, source_target_pairs={{8,0},{16,8},{24,16},{32,24},{40,32},{48,40},{56,48},{64,56},{72,6... | collective-permute-start | bytes 24584 | tf_op jit(solution)/shard_map/ppermute | solution.py:61
  232.5 8.6 %collective-permute-start.11 = (f32[1,16,128]{2,1,0:T(8,128)S(1)}, f32[1,16,128]{2,1,0:T(8,128)S(1)}, u32[]{:S(2)}, u32[]{:S(2)}) collective-permute-start(f32[1,16,128]{2,1,0:T(8,128)S(1)} %fusion.213), channel_id=1, source_target_pairs={{0,8},{8,16},{16,24},{24,32},{32,40},{40,48},{48,56},{56,64},{64,7... | collective-permute-start | bytes 24584 | tf_op jit(solution)/shard_map/ppermute | solution.py:60
  236.6 4.6 %collective-permute-start.13 = (f32[1,1,128]{2,1,0:T(1,128)S(1)}, f32[1,1,128]{2,1,0:T(1,128)S(1)}, u32[]{:S(2)}, u32[]{:S(2)}) collective-permute-start(f32[1,1,128]{2,1,0:T(1,128)S(1)} %get-tuple-element.82), channel_id=1, source_target_pairs={{0,1},{1,2},{2,3},{3,4},{4,5},{5,6},{6,7},{8,9},{9,10},{10,11},{11... | collective-permute-start | bytes 1544 | tf_op jit(solution)/shard_map/ppermute | solution.py:60
  239.2 7.0 %collective-permute-start.12 = (f32[1,1,128]{2,1,0:T(1,128)S(1)}, f32[1,1,128]{2,1,0:T(1,128)S(1)}, u32[]{:S(2)}, u32[]{:S(2)}) collective-permute-start(f32[1,1,128]{2,1,0:T(1,128)S(1)} %get-tuple-element.81), channel_id=1, source_target_pairs={{1,0},{2,1},{3,2},{4,3},{5,4},{6,5},{7,6},{9,8},{10,9},{11,10},{12... | collective-permute-start | bytes 1544 | tf_op jit(solution)/shard_map/ppermute | solution.py:61
  246.3 9.9 %collective-permute-start.14 = (f32[1,16,128]{2,1,0:T(8,128)S(1)}, f32[1,16,128]{2,1,0:T(8,128)S(1)}, u32[]{:S(2)}, u32[]{:S(2)}) collective-permute-start(f32[1,16,128]{2,1,0:T(8,128)S(1)} %fusion.209), channel_id=1, source_target_pairs={{8,0},{16,8},{24,16},{32,24},{40,32},{48,40},{56,48},{64,56},{72,6... | collective-permute-start | bytes 24584 | tf_op jit(solution)/shard_map/ppermute | solution.py:61
  247.6 8.6 %collective-permute-start.15 = (f32[1,16,128]{2,1,0:T(8,128)S(1)}, f32[1,16,128]{2,1,0:T(8,128)S(1)}, u32[]{:S(2)}, u32[]{:S(2)}) collective-permute-start(f32[1,16,128]{2,1,0:T(8,128)S(1)} %fusion.209), channel_id=1, source_target_pairs={{0,8},{8,16},{16,24},{24,32},{32,40},{40,48},{48,56},{56,64},{64,7... | collective-permute-start | bytes 24584 | tf_op jit(solution)/shard_map/ppermute | solution.py:60
  251.7 4.6 %collective-permute-start.17 = (f32[1,1,128]{2,1,0:T(1,128)S(1)}, f32[1,1,128]{2,1,0:T(1,128)S(1)}, u32[]{:S(2)}, u32[]{:S(2)}) collective-permute-start(f32[1,1,128]{2,1,0:T(1,128)S(1)} %get-tuple-element.80), channel_id=1, source_target_pairs={{0,1},{1,2},{2,3},{3,4},{4,5},{5,6},{6,7},{8,9},{9,10},{10,11},{11... | collective-permute-start | bytes 1544 | tf_op jit(solution)/shard_map/ppermute | solution.py:60
  254.2 7.0 %collective-permute-start.16 = (f32[1,1,128]{2,1,0:T(1,128)S(1)}, f32[1,1,128]{2,1,0:T(1,128)S(1)}, u32[]{:S(2)}, u32[]{:S(2)}) collective-permute-start(f32[1,1,128]{2,1,0:T(1,128)S(1)} %get-tuple-element.79), channel_id=1, source_target_pairs={{1,0},{2,1},{3,2},{4,3},{5,4},{6,5},{7,6},{9,8},{10,9},{11,10},{12... | collective-permute-start | bytes 1544 | tf_op jit(solution)/shard_map/ppermute | solution.py:61
  262.9 22.6 %copy-start.12 = (s32[3]{0:T(128)S(1)}, s32[3]{0:T(128)}, u32[]{:S(2)}) copy-start(s32[3]{0:T(128)} %constant.316.clone.1) | copy-start | bytes 40
  262.9 32.3 %all-to-all-start.1 = ((f32[64,1,16,128]{3,2,1,0:T(8,128)}), f32[64,1,16,128]{3,2,1,0:T(8,128)S(1)}, u32[]{:S(2)}, u32[]{:S(2)}) async-start(f32[64,1,16,128]{3,2,1,0:T(8,128)} %broadcast_in_dim.155), calls=%async_computation.1 | async-start | bytes 1048576 | tf_op jit(solution)/shard_map/all_to_all | solution.py:74
  280.5 5.8 %collective-permute-start.18 = (f32[64,4,128]{2,1,0:T(4,128)S(1)}, f32[64,4,128]{2,1,0:T(4,128)S(1)}, u32[]{:S(2)}, u32[]{:S(2)}) collective-permute-start(f32[64,4,128]{2,1,0:T(4,128)S(1)} %get-tuple-element.78), channel_id=1, source_target_pairs={{0,1},{1,2},{2,3},{3,4},{4,5},{5,6},{6,7},{8,9},{9,10},{10,11},{11... | collective-permute-start | bytes 393224 | tf_op jit(solution)/shard_map/ppermute | solution.py:24
  282.8 10.2 %collective-permute-start.19 = (f32[64,4,128]{2,1,0:T(4,128)S(1)}, f32[64,4,128]{2,1,0:T(4,128)}, u32[]{:S(2)}, u32[]{:S(2)}) collective-permute-start(f32[64,4,128]{2,1,0:T(4,128)S(1)} %get-tuple-element.77), channel_id=1, source_target_pairs={{1,0},{2,1},{3,2},{4,3},{5,4},{6,5},{7,6},{9,8},{10,9},{11,10},{12... | collective-permute-start | bytes 393224 | tf_op jit(solution)/shard_map/ppermute | solution.py:27
  305.8 15.0 %copy-start.3 = (f32[64,16,128]{2,1,0:T(8,128)S(1)}, f32[64,16,128]{2,1,0:T(8,128)}, u32[]{:S(2)}) copy-start(f32[64,16,128]{2,1,0:T(8,128)} %scatter-add.52) | copy-start | bytes 1572868
  306.9 5.0 %collective-permute-start.20 = (f32[64,4,128]{2,1,0:T(4,128)S(1)}, f32[64,4,128]{2,1,0:T(4,128)S(1)}, u32[]{:S(2)}, u32[]{:S(2)}) collective-permute-start(f32[64,4,128]{2,1,0:T(4,128)S(1)} %get-tuple-element.76), channel_id=1, source_target_pairs={{0,1},{1,2},{2,3},{3,4},{4,5},{5,6},{6,7},{8,9},{9,10},{10,11},{11... | collective-permute-start | bytes 393224 | tf_op jit(solution)/shard_map/ppermute | solution.py:24
  308.8 10.1 %collective-permute-start.21 = (f32[64,4,128]{2,1,0:T(4,128)S(1)}, f32[64,4,128]{2,1,0:T(4,128)S(1)}, u32[]{:S(2)}, u32[]{:S(2)}) collective-permute-start(f32[64,4,128]{2,1,0:T(4,128)S(1)} %get-tuple-element.75), channel_id=1, source_target_pairs={{1,0},{2,1},{3,2},{4,3},{5,4},{6,5},{7,6},{9,8},{10,9},{11,10},{12... | collective-permute-start | bytes 393224 | tf_op jit(solution)/shard_map/ppermute | solution.py:27
  (9 other events, 22.9 us)
where the time goes:
time: 329 us; the launch traced here: 327 us
  starting transfers between devices  102 us (31%)
  other arithmetic  98.1 us (30%)
  waiting for transfers between devices  83.9 us (26%)
  local copies, waits for them, and re-layouts  28.3 us (9%)
  between operations  14.8 us (4%)
    ppermute x3, waiting for transfers between devices, with_halo(): lax.ppermute(lax.slice_in_dim(block, 0, width, axis=dim), axis, backward)  46.8 us
    ppermute x8, starting transfers between devices, padded_2(): lax.ppermute(last, axis, up)  42.4 us
    scatter-add x3, other arithmetic, local(): following.at[1, band_receiver[0], band_receiver[1], band_receiver[2]]  38.2 us
    select_n x3, other arithmetic, local(): following = jnp.where(valid, following, 0.0)  34.4 us
    ppermute x8, waiting for transfers between devices, padded_2(): lax.ppermute(initial, axis, [(b, a) for a, b in up])  18.9 us
    all_to_all x1, waiting for transfers between devices, sent_and_summed(): lax.all_to_all(blocks, axis, split_axis=0, concat_axis=0, tiled=True)  17.8 us
    all_to_all x1, starting transfers between devices, copy_for_each(): return lax.all_to_all(copies, axis, split_axis=0, concat_axis=0, tiled=True)  16.7 us
    ppermute x3, starting transfers between devices, with_halo(): lax.ppermute(lax.slice_in_dim(block, 0, width, axis=dim), axis, backward)  13.3 us
  transfers between devices with their start and end apart: 24, of which 9 were waited for; matrix products, arithmetic and copies ran while one was open for 4% of the time, Pallas kernels for 0%

commit v1 on v0

v1 whole, which is shorter than its diff:
```python
import functools

import jax
import jax.numpy as jnp
from jax import lax
from jax.experimental import pallas as pl
from jax.experimental.pallas import tpu as pltpu
from jax.sharding import PartitionSpec as P

MESH = pl.DeviceIdType.MESH
STEPS = 3
FINAL = 2
PASSES = 4
RDEPTH = 2
LANES = 128
H = 4
PAD = 8

stencil_weights = (-205.0 / 72.0, 8.0 / 5.0, -1.0 / 5.0, 8.0 / 315.0, -1.0 / 560.0)
diffuse_rate = 0.1
step_length = 0.1
speed_floor = 0.16
speed_ceiling = 0.44


def kernel(
    sizes,
    source_cell,
    wavelet,
    receiver_cell,
    residual,
    wave_prev,
    wave_now,
    adjoint_prev,
    adjoint_now,
    velocity,
    wave_out,
    adjoint_out,
    speed_out,
    staged,
    U,
    W,
    speed,
    square,
    received,
    G,
    I,
    rx,
    rz,
    ry,
    sx,
    sz,
    F,
    FA,
    FB,
    L,
    outs,
    in_sem,
    out_sem,
    halo_send,
    halo_recv,
    rs_send,
    rs_recv,
    ag_send,
    ag_recv,
):
    X, Z, Y, boxes, NX, R = sizes
    NY = R * boxes
    q, h, c = R // X, R // (X * Z), NX // Y
    shot, box = lax.axis_index("shot"), lax.axis_index("box")
    x = lax.div(shot, Z * Y)
    z = lax.rem(lax.div(shot, Y), Z)
    y = lax.rem(shot, Y)
    lower, upper = lax.max(box - 1, 0), lax.min(box + 1, boxes - 1)
    has_lower, has_upper = box > 0, box < boxes - 1

    def peer_x(d):
        return (lax.rem(x + d, X) * Z + z) * Y + y

    def peer_z(d):
        return (x * Z + lax.rem(z + d, Z)) * Y + y

    def peer_y(d):
        return (x * Z + z) * Y + lax.rem(y + d, Y)

    loads = [
        pltpu.make_async_copy(ref, staged.at[i], in_sem.at[i])
        for i, ref in enumerate((wave_now, adjoint_now, wave_prev, adjoint_prev, velocity))
    ]
    for load in loads:
        load.start()

    barrier = pltpu.get_barrier_semaphore()
    peers = (
        [peer_x(d) for d in range(1, X)]
        + [peer_z(d) for d in range(1, Z)]
        + [peer_y(d) for d in range(1, Y)]
    )
    for peer in peers:
        pl.semaphore_signal(barrier, inc=1, device_id={"shot": peer}, device_id_type=MESH)

    @pl.when(has_lower)
    def _():
        pl.semaphore_signal(barrier, inc=1, device_id={"box": lower}, device_id_type=MESH)

    @pl.when(has_upper)
    def _():
        pl.semaphore_signal(barrier, inc=1, device_id={"box": upper}, device_id_type=MESH)

    pad = jnp.zeros((R, PAD, LANES), jnp.float32)
    edge = jnp.zeros((H, NX, LANES), jnp.float32)
    for fields, slots in ((U, range(1, 6)), (W, range(1, 4))):
        for slot in slots:
            fields[slot, H : H + R, :PAD, :] = pad
            fields[slot, H : H + R, PAD + NX :, :] = pad

    @pl.when(box == 0)
    def _():
        for fields, slots in ((U, range(1, 6)), (W, range(1, 4))):
            for slot in slots:
                fields[slot, :H, PAD : PAD + NX, :] = edge
        F[:H] = edge

    @pl.when(box == boxes - 1)
    def _():
        for fields, slots in ((U, range(1, 6)), (W, range(1, 4))):
            for slot in slots:
                fields[slot, H + R :, PAD : PAD + NX, :] = edge
        F[H + R :] = edge

    class Halo:
        def __init__(self, ref, index, padded=True):
            def rows(start):
                if padded:
                    return ref.at[pl.ds(start, H), pl.ds(PAD, NX), :]
                return ref.at[pl.ds(start, H)]

            self.down = pltpu.make_async_remote_copy(
                src_ref=rows(H),
                dst_ref=rows(H + R),
                send_sem=halo_send.at[index, 0],
                recv_sem=halo_recv.at[index, 0],
                device_id={"box": lower},
                device_id_type=MESH,
            )
            self.up = pltpu.make_async_remote_copy(
                src_ref=rows(R),
                dst_ref=rows(0),
                send_sem=halo_send.at[index, 1],
                recv_sem=halo_recv.at[index, 1],
                device_id={"box": upper},
                device_id_type=MESH,
            )

        def start(self):
            pl.when(has_lower)(self.down.start)
            pl.when(has_upper)(self.up.start)

        def arrive(self):
            pl.when(has_lower)(self.up.wait_recv)
            pl.when(has_upper)(self.down.wait_recv)

        def leave(self):
            pl.when(has_lower)(self.down.wait_send)
            pl.when(has_upper)(self.up.wait_send)

    halo_u = {t: Halo(U.at[t], t - 1) for t in range(1, 6)}
    halo_w = {t: Halo(W.at[t], 4 + t) for t in range(1, 4)}
    halo_f = Halo(F, 8, padded=False)

    lane = lax.broadcasted_iota(jnp.int32, (1, LANES), 1)
    first = lax.broadcasted_iota(jnp.int32, (NX, 1), 0)
    flat = lax.broadcasted_iota(jnp.int32, (NX, LANES), 0) * (NY * LANES) + lax.broadcasted_iota(
        jnp.int32, (NX, LANES), 1
    )
    start_second = box * R
    source = source_cell[0]

    def over(begin, end, body):
        lax.fori_loop(begin, end, lambda r, carry: (body(r), carry)[1], 0)

    def over_edges(body):
        def step(i, carry):
            body(jnp.where(i < H, i, i + (R - 2 * H)))
            return carry

        lax.fori_loop(0, 2 * H, step, 0)

    def turned(i, r):
        return staged[i, pl.ds(r, NX, stride=R), :]

    def centre(r):
        return (H + r, pl.ds(PAD, NX), slice(None))

    def laplace(ref, r):
        field = ref[centre(r)]
        summed = (3.0 * stencil_weights[0]) * field
        for k in range(1, 5):
            weight = stencil_weights[k]
            around = (ref[H + r + k, pl.ds(PAD, NX), :] + ref[H + r - k, pl.ds(PAD, NX), :]) + (
                ref[H + r, pl.ds(PAD + k, NX), :] + ref[H + r, pl.ds(PAD - k, NX), :]
            )
            summed = summed + weight * around
            summed = summed + jnp.where(lane >= k, weight, 0.0) * pltpu.roll(field, k, 1)
            summed = summed + jnp.where(lane < LANES - k, weight, 0.0) * pltpu.roll(field, LANES - k, 1)
        return field, summed

    def injected(r, amplitude):
        return jnp.where(flat == source - (start_second + r) * LANES, amplitude, 0.0)

    pl.semaphore_wait(
        barrier, len(peers) + has_lower.astype(jnp.int32) + has_upper.astype(jnp.int32)
    )
    loads[0].wait()

    def turn_wave(r):
        U[(1, *centre(r))] = turned(0, r)

    over(0, R, turn_wave)
    halo_u[1].start()
    loads[1].wait()

    def turn_adjoint(r):
        W[(1, *centre(r))] = turned(1, r)

    over(0, R, turn_adjoint)
    halo_w[1].start()
    loads[2].wait()
    loads[3].wait()
    loads[4].wait()

    def turn_rest(r):
        U[(0, *centre(r))] = turned(2, r)
        W[(0, *centre(r))] = turned(3, r)
        v = turned(4, r)
        speed[r] = v
        square[r] = v * v
        here = (first * NY + (start_second + r)) * LANES + RDEPTH
        picks = jnp.where(receiver_cell[...] == here, 1.0, 0.0)
        for t in range(STEPS):
            sub = lax.broadcasted_iota(jnp.int32, (LANES, LANES), 0)
            values = jnp.where(sub == RDEPTH, residual[t : t + 1, :], 0.0)
            received[t, r] = lax.dot_general(
                picks,
                values,
                (((1,), (1,)), ((), ())),
                precision=lax.Precision.HIGHEST,
                preferred_element_type=jnp.float32,
            )

    over(0, R, turn_rest)

    def wave_row(t):
        now, early, later = U.at[t], U.at[t - 1], U.at[t + 1]
        amplitude = wavelet[0, t - 1]

        def body(r):
            field, summed = laplace(now, r)
            second_diff = square[r] * summed + injected(r, amplitude)
            later[centre(r)] = (2.0 * field - early[centre(r)]) + second_diff
            term = W[(t, *centre(r))] * second_diff
            G[r] = term if t == 1 else G[r] + term

        return body

    def adjoint_row(t, last=False):
        now, early = W.at[t], W.at[t - 1]

        def body(r):
            field, summed = laplace(now, r)
            value = (2.0 * field - early[centre(r)]) + (square[r] * summed + received[t - 1, r])
            if last:
                outs[1, pl.ds(r, NX, stride=R), :] = value
            else:
                W[(t + 1, *centre(r))] = value

        return body

    class Reduce:
        def __init__(self, which, ref):
            self.ref, self.which = ref, which
            self.x = []
            for d in range(1, X):
                target = lax.rem(x + d, X)
                self.x.append(self.copy(d - 1, ref.at[pl.ds(target * q, q)], rx.at[which, d - 1], peer_x(d)))
            self.z = []
            for d in range(1, Z):
                target = lax.rem(z + d, Z)
                self.z.append(
                    self.copy(X + d - 2, sx.at[which, pl.ds(target * h, h)], rz.at[which, d - 1], peer_z(d))
                )
            self.y = []
            for d in range(1, Y):
                target = lax.rem(y + d, Y)
                self.y.append(
                    self.copy(
                        X + Z + d - 3,
                        sz.at[which, :, pl.ds(pl.multiple_of(target * c, c), c), :],
                        ry.at[which, d - 1],
                        peer_y(d),
                    )
                )

        def copy(self, index, src, dst, peer):
            return pltpu.make_async_remote_copy(
                src_ref=src,
                dst_ref=dst,
                send_sem=rs_send.at[self.which, index],
                recv_sem=rs_recv.at[self.which, index],
                device_id={"shot": peer},
                device_id_type=MESH,
            )

        def start_x(self):
            for copy in self.x:
                copy.start()

        def then_z(self):
            for copy in self.x:
                copy.wait_recv()

            def add(r):
                total = self.ref[x * q + r]
                for d in range(1, X):
                    total = total + rx[self.which, d - 1, r]
                sx[self.which, r] = total

            over(0, q, add)
            for copy in self.z:
                copy.start()

        def then_y(self):
            for copy in self.z:
                copy.wait_recv()

            def add(r):
                total = sx[self.which, z * h + r]
                for d in range(1, Z):
                    total = total + rz[self.which, d - 1, r]
                sz[self.which, r] = total

            over(0, h, add)
            for copy in self.y:
                copy.start()

        def piece(self):
            for copy in self.y:
                copy.wait_recv()
            total = sz[self.which, :, pl.ds(pl.multiple_of(y * c, c), c), :]
            for d in range(1, Y):
                total = total + ry[self.which, d - 1]
            return total

        def leave(self):
            for copy in self.x + self.z + self.y:
                copy.wait_send()

    reduce_g, reduce_i = Reduce(0, G), Reduce(1, I)

    for t in range(1, STEPS):
        over(H, R - H, wave_row(t))
        halo_u[t].arrive()
        over_edges(wave_row(t))
        halo_u[t + 1].start()
        over(H, R - H, adjoint_row(t))
        halo_w[t].arrive()
        over_edges(adjoint_row(t))
        halo_w[t + 1].start()

    def light(r):
        one, two, three = (U[(t, *centre(r))] for t in range(1, 4))
        I[r] = (one * one + two * two) + three * three

    over(0, R, light)
    reduce_i.start_x()
    over(H, R - H, wave_row(STEPS))
    halo_u[STEPS].arrive()
    over_edges(wave_row(STEPS))
    halo_u[STEPS + 1].start()
    reduce_g.start_x()
    reduce_i.then_z()
    over(H, R - H, adjoint_row(STEPS, last=True))
    halo_w[STEPS].arrive()
    over_edges(adjoint_row(STEPS, last=True))
    adjoint_store = pltpu.make_async_copy(outs.at[1], adjoint_out, out_sem.at[1])
    adjoint_store.start()
    reduce_i.then_y()

    reduce_g.then_z()

    def last_laplace(r):
        L[r] = laplace(U.at[STEPS + 1], r)[1]

    over(H, R - H, last_laplace)
    reduce_g.then_y()
    halo_u[STEPS + 1].arrive()
    over_edges(last_laplace)
    illumination = reduce_i.piece()
    gradient = reduce_g.piece()

    row = H + x * q + z * h
    F[pl.ds(row, h), pl.ds(pl.multiple_of(y * c, c), c), :] = gradient / jnp.sqrt(illumination + 1.0)

    def share(index, part, peer):
        return pltpu.make_async_remote_copy(
            src_ref=part,
            dst_ref=part,
            send_sem=ag_send.at[index],
            recv_sem=ag_recv.at[index],
            device_id={"shot": peer},
            device_id_type=MESH,
        )

    part_y = F.at[pl.ds(row, h), pl.ds(pl.multiple_of(y * c, c), c), :]
    shares = [share(X + Z + d - 3, part_y, peer_y(d)) for d in range(1, Y)]
    for copy in shares:
        copy.start()
    for copy in shares:
        copy.wait_recv()
    sent = shares
    part_z = F.at[pl.ds(row, h)]
    shares = [share(X + d - 2, part_z, peer_z(d)) for d in range(1, Z)]
    for copy in shares:
        copy.start()
    for copy in shares:
        copy.wait_recv()
    sent = sent + shares
    part_x = F.at[pl.ds(H + x * q, q)]
    shares = [share(d - 1, part_x, peer_x(d)) for d in range(1, X)]
    for copy in shares:
        copy.start()
    for copy in shares:
        copy.wait_recv()
    sent = sent + shares
    halo_f.start()
    halo_f.arrive()

    def conduct(rise):
        return rise / (1.0 + rise * rise)

    def diffuse(src, last, put):
        def face(r, rise):
            at = start_second + (r - H)
            return jnp.where((at > 0) & (at < NY), conduct(rise), 0.0)

        begin, end = last + 1, R + 2 * H - 1 - last

        def body(r, carry):
            below, field = carry
            higher = src[r + 1]
            above = face(r + 1, higher - field)
            along_first = jnp.where(first < NX - 1, conduct(pltpu.roll(field, NX - 1, 0) - field), 0.0)
            along_third = jnp.where(lane < LANES - 1, conduct(pltpu.roll(field, LANES - 1, 1) - field), 0.0)
            change = (
                (along_first - pltpu.roll(along_first, 1, 0))
                + (above - below)
                + (along_third - pltpu.roll(along_third, 1, 1))
            )
            put(r, field + diffuse_rate * change)
            return above, higher

        field = src[begin]
        lax.fori_loop(begin, end, body, (face(begin, field - src[begin - 1]), field))

    def into(ref):
        def put(r, value):
            ref[r] = value

        return put

    def update(r, value):
        new_speed = jnp.clip(speed[r - H] - step_length * value, speed_floor, speed_ceiling)
        outs[2, pl.ds(r - H, NX, stride=R), :] = new_speed
        square[r - H] = new_speed * new_speed

    diffuse(F, 0, into(FA))
    diffuse(FA, 1, into(FB))
    diffuse(FB, 2, into(FA))
    diffuse(FA, 3, update)
    speed_store = pltpu.make_async_copy(outs.at[2], speed_out, out_sem.at[2])
    speed_store.start()

    def final_one(r):
        value = (2.0 * U[(STEPS + 1, *centre(r))] - U[(STEPS, *centre(r))]) + (
            square[r] * L[r] + injected(r, wavelet[0, STEPS])
        )
        U[(STEPS + 2, *centre(r))] = value

    def final_two(r):
        field, summed = laplace(U.at[STEPS + 2], r)
        outs[0, pl.ds(r, NX, stride=R), :] = (2.0 * field - U[(STEPS + 1, *centre(r))]) + (
            square[r] * summed + injected(r, wavelet[0, STEPS + 1])
        )

    over_edges(final_one)
    halo_u[STEPS + 2].start()
    over(H, R - H, final_one)
    over(H, R - H, final_two)
    halo_u[STEPS + 2].arrive()
    over_edges(final_two)
    wave_store = pltpu.make_async_copy(outs.at[0], wave_out, out_sem.at[0])
    wave_store.start()

    for halo in (*halo_u.values(), *halo_w.values(), halo_f):
        halo.leave()
    reduce_g.leave()
    reduce_i.leave()
    for copy in sent:
        copy.wait_send()
    adjoint_store.wait()
    speed_store.wait()
    wave_store.wait()


def local(
    parts,
    boxes,
    wave_prev,
    wave_now,
    adjoint_prev,
    adjoint_now,
    velocity,
    source_cell,
    wavelet,
    receiver_cell,
    residual,
):
    X, Z, Y = parts
    NX, R, D = velocity.shape
    q, h, c = R // X, R // (X * Z), NX // Y
    f32 = jnp.float32
    flat = (NX * R, D)
    padded = (R + 2 * H, NX + 2 * PAD, D)
    plain = (R, NX, D)
    around = (R + 2 * H, NX, D)
    n_rs = X + Y + Z - 3
    vmem, smem, anywhere = (
        pl.BlockSpec(memory_space=pltpu.VMEM),
        pl.BlockSpec(memory_space=pltpu.SMEM),
        pl.BlockSpec(memory_space=pl.ANY),
    )
    out = jax.ShapeDtypeStruct(flat, f32)
    wave_out, adjoint_out, speed_out = pl.pallas_call(
        functools.partial(kernel, (X, Z, Y, boxes, NX, R)),
        out_shape=(out, out, out),
        in_specs=[smem, smem, vmem, vmem] + [anywhere] * 5,
        out_specs=(anywhere, anywhere, anywhere),
        scratch_shapes=[
            pltpu.VMEM((5, *flat), f32),
            pltpu.VMEM((6, *padded), f32),
            pltpu.VMEM((4, *padded), f32),
            pltpu.VMEM(plain, f32),
            pltpu.VMEM(plain, f32),
            pltpu.VMEM((STEPS, *plain), f32),
            pltpu.VMEM(plain, f32),
            pltpu.VMEM(plain, f32),
            pltpu.VMEM((2, max(X - 1, 1), q, NX, D), f32),
            pltpu.VMEM((2, max(Z - 1, 1), h, NX, D), f32),
            pltpu.VMEM((2, max(Y - 1, 1), h, c, D), f32),
            pltpu.VMEM((2, q, NX, D), f32),
            pltpu.VMEM((2, h, NX, D), f32),
            pltpu.VMEM(around, f32),
            pltpu.VMEM(around, f32),
            pltpu.VMEM(around, f32),
            pltpu.VMEM(plain, f32),
            pltpu.VMEM((3, *flat), f32),
            pltpu.SemaphoreType.DMA((5,)),
            pltpu.SemaphoreType.DMA((3,)),
            pltpu.SemaphoreType.DMA((9, 2)),
            pltpu.SemaphoreType.DMA((9, 2)),
            pltpu.SemaphoreType.DMA((2, n_rs)),
            pltpu.SemaphoreType.DMA((2, n_rs)),
            pltpu.SemaphoreType.DMA((n_rs,)),
            pltpu.SemaphoreType.DMA((n_rs,)),
        ],
        compiler_params=pltpu.CompilerParams(
            collective_id=0, has_side_effects=True, vmem_limit_bytes=56 * 1024 * 1024
        ),
    )(
        source_cell,
        wavelet,
        receiver_cell,
        residual.reshape(residual.shape[1:]),
        wave_prev.reshape(flat),
        wave_now.reshape(flat),
        adjoint_prev.reshape(flat),
        adjoint_now.reshape(flat),
        velocity.reshape(flat),
    )
    field = (1, NX, R, D)
    return wave_out.reshape(field), adjoint_out.reshape(field), speed_out.reshape(field[1:])


def solution(mesh):
    shots, boxes = mesh.shape["shot"], mesh.shape["box"]
    parts = {64: (4, 2, 8), 16: (4, 2, 2), 8: (4, 2, 1)}[shots]
    return jax.shard_map(
        functools.partial(local, parts, boxes),
        mesh=mesh,
        in_specs=(
            P("shot", None, "box", None),
            P("shot", None, "box", None),
            P("shot", None, "box", None),
            P("shot", None, "box", None),
            P(None, "box", None),
            P("shot"),
            P("shot", None),
            P("shot", None),
            P("shot", None, None),
        ),
        out_specs=(
            P("shot", None, "box", None),
            P("shot", None, "box", None),
            P(None, "box", None),
        ),
        check_vma=False,
    )
```

time: 329 us -> 95.1 us (0.29)
  starting transfers between devices: 102 us -> 0 us
  other arithmetic: 98.1 us -> 0 us
  Pallas kernels: 0 us -> 88.4 us
  waiting for transfers between devices: 83.9 us -> 0 us
  local copies, waits for them, and re-layouts: 28.3 us -> 5.2 us
  between operations: 14.8 us -> 1.3 us
    pallas_call x0 -> x1, Pallas kernels: none -> 88.4 us  [local(): pl.pallas_call(functools.partial(kernel, (X, Z, Y, boxes, NX, R)), out_sh...]
    ppermute x22 -> x0, starting transfers between devices: 74.6 us -> none  [the longest x8 42.4 us: padded_2(): lax.ppermute(last, axis, up)]
    ppermute x22 -> x0, waiting for transfers between devices: 65.8 us -> none  [the longest x3 46.8 us: with_halo(): lax.ppermute(lax.slice_in_dim(block, 0, width, axis=dim), axis, backward)]
    scatter-add x3 -> x0, other arithmetic: 38.2 us -> none  [local(): following.at[1, band_receiver[0], band_receiver[1], band_receiver[2]]]
    select_n x13 -> x0, other arithmetic: 35 us -> none  [the longest x3 34.4 us: local(): following = jnp.where(valid, following, 0.0)]
    all_to_all x2 -> x0, starting transfers between devices: 27.1 us -> none  [the longest x1 16.7 us: copy_for_each(): return lax.all_to_all(copies, axis, split_axis=0, concat_axis=0, tiled=True)]
    all_to_all x2 -> x0, waiting for transfers between devices: 18.2 us -> none  [the longest x1 17.8 us: sent_and_summed(): lax.all_to_all(blocks, axis, split_axis=0, concat_axis=0, tiled=True)]
    add x9 -> x0, other arithmetic: 13.4 us -> none  [the longest x2 8.41 us: local(): following = 2.0 * wave_current - wave_earlier + new_square * laplace(padded)]
  transfers between devices with their start and end apart: 24 -> 0, of which waited for: 9 -> 0; matrix products, arithmetic and copies ran while one was open for 4% -> 0% of each run, Pallas kernels for 0% -> 0%
where the time goes in v1:
time: 95.1 us; the launch traced here: 94.9 us
  Pallas kernels  88.4 us (93%)
  local copies, waits for them, and re-layouts  5.2 us (5%)
  between operations  1.3 us (1%)
    pallas_call x1, Pallas kernels, local(): pl.pallas_call(functools.partial(kernel, (X, Z, Y, boxes, NX, R)), out_sh...  88.4 us
    unnamed x10, local copies, waits for them, and re-layouts  5.2 us

profile of v1, /device:TPU:1, one launch (start us, length us, event | category | flops | bytes accessed | tf_op | source)
XLA Modules:
  0.0 94.9 jit_solution(2700320325709330631)
XLA Ops:
  1.3 0.0 copy-start.2
  1.3 0.7 copy-done.2
  2.0 0.6 copy.14
  2.5 88.4 %shard_map.112 = (f32[1024,128]{1,0:T(8,128)}, f32[1024,128]{1,0:T(8,128)}, f32[1024,128]{1,0:T(8,128)}) custom-call(s32[1]{0:T(128)S(6)} %copy.18.source_cell, f32[1,5]{1,0:T(1,128)} %wavelet.1, s32[1,128]{1,0:T(1,128)} %receiver_cell.1, f32[3,128]{1,0:T(4,128)} %bitcast.19, f32[1024,128]{1,0:T(8,128)} %bitcast.14, f32[1024,128]{1,0:T(8,128)} %bitcast.15, ...), custom_call_target="tpu_custom_call" | custom-call | tf_op jit(solution)/shard_map/pallas_call | solution.py:543
  90.9 0.0 copy-start.1
  90.9 1.9 %copy.19 = f32[1,64,16,128]{3,2,1,0:T(8,128)} copy(f32[1,64,16,128]{3,2,1,0:T(8,128)} %bitcast.13) | data formatting | bytes 1048576
  92.8 0.0 copy-done.1
  92.8 0.0 copy-start
  92.8 0.8 copy.20
  93.6 0.4 copy-done
  94.1 0.8 copy.21
Async XLA Ops:
  1.3 0.7 copy-start.2
  90.9 1.9 %copy-start.1 = (f32[1024,128]{1,0:T(8,128)S(1)}, f32[1024,128]{1,0:T(8,128)}, u32[]{:S(2)}) copy-start(f32[1024,128]{1,0:T(8,128)} %get-tuple-element.7) | copy-start | bytes 1572868
  92.8 1.2 %copy-start = (f32[1024,128]{1,0:T(8,128)S(1)}, f32[1024,128]{1,0:T(8,128)}, u32[]{:S(2)}) copy-start(f32[1024,128]{1,0:T(8,128)} %get-tuple-element.8) | copy-start | bytes 1572868

commit v2 on v1

--- a/solution.py
+++ b/solution.py
@@ -50,10 +50,11 @@
     ry,
     sx,
     sz,
-    F,
-    FA,
-    FB,
+    E,
+    S,
     L,
+    zu,
+    zw,
     outs,
     in_sem,
     out_sem,
@@ -63,6 +64,8 @@
     rs_recv,
     ag_send,
     ag_recv,
+    near_send,
+    near_recv,
 ):
     X, Z, Y, boxes, NX, R = sizes
     NY = R * boxes
@@ -83,6 +86,24 @@
     def peer_y(d):
         return (x * Z + z) * Y + lax.rem(y + d, Y)
 
+    pieces = X * Z
+    place = box * pieces + x * Z + z
+    reach = -(-H // h)
+    beside = [e for e in (-1, 0, 1) if Y > 1 or e == 0]
+    near = [(d, e) for d in range(-reach, reach + 1) for e in beside if (d, e) != (0, 0)]
+
+    def is_near(d, e):
+        return (place + d >= 0) & (place + d < boxes * pieces) & (y + e >= 0) & (y + e < Y)
+
+    def owner(d, e):
+        other = lax.clamp(0, place + d, boxes * pieces - 1)
+        return {
+            "shot": lax.rem(other, pieces) * Y + lax.clamp(0, y + e, Y - 1),
+            "box": lax.div(other, pieces),
+        }
+
+    E[...] = jnp.zeros_like(E)
+
     loads = [
         pltpu.make_async_copy(ref, staged.at[i], in_sem.at[i])
         for i, ref in enumerate((wave_now, adjoint_now, wave_prev, adjoint_prev, velocity))
@@ -107,6 +128,15 @@
     def _():
         pl.semaphore_signal(barrier, inc=1, device_id={"box": upper}, device_id_type=MESH)
 
+    count = len(peers) + has_lower.astype(jnp.int32) + has_upper.astype(jnp.int32)
+    for d, e in near:
+
+        @pl.when(is_near(d, e))
+        def _(d=d, e=e):
+            pl.semaphore_signal(barrier, inc=1, device_id=owner(d, e), device_id_type=MESH)
+
+        count = count + is_near(d, e).astype(jnp.int32)
+
     pad = jnp.zeros((R, PAD, LANES), jnp.float32)
     edge = jnp.zeros((H, NX, LANES), jnp.float32)
     for fields, slots in ((U, range(1, 6)), (W, range(1, 4))):
@@ -119,21 +149,17 @@
         for fields, slots in ((U, range(1, 6)), (W, range(1, 4))):
             for slot in slots:
                 fields[slot, :H, PAD : PAD + NX, :] = edge
-        F[:H] = edge
 
     @pl.when(box == boxes - 1)
     def _():
         for fields, slots in ((U, range(1, 6)), (W, range(1, 4))):
             for slot in slots:
                 fields[slot, H + R :, PAD : PAD + NX, :] = edge
-        F[H + R :] = edge
 
     class Halo:
-        def __init__(self, ref, index, padded=True):
+        def __init__(self, ref, index):
             def rows(start):
-                if padded:
-                    return ref.at[pl.ds(start, H), pl.ds(PAD, NX), :]
-                return ref.at[pl.ds(start, H)]
+                return ref.at[pl.ds(start, H), pl.ds(PAD, NX), :]
 
             self.down = pltpu.make_async_remote_copy(
                 src_ref=rows(H),
@@ -166,7 +192,6 @@
 
     halo_u = {t: Halo(U.at[t], t - 1) for t in range(1, 6)}
     halo_w = {t: Halo(W.at[t], 4 + t) for t in range(1, 4)}
-    halo_f = Halo(F, 8, padded=False)
 
     lane = lax.broadcasted_iota(jnp.int32, (1, LANES), 1)
     first = lax.broadcasted_iota(jnp.int32, (NX, 1), 0)
@@ -192,25 +217,63 @@
     def centre(r):
         return (H + r, pl.ds(PAD, NX), slice(None))
 
-    def laplace(ref, r):
-        field = ref[centre(r)]
-        summed = (3.0 * stencil_weights[0]) * field
+    apart = lax.broadcasted_iota(jnp.int32, (LANES, LANES), 0) - lax.broadcasted_iota(
+        jnp.int32, (LANES, LANES), 1
+    )
+    along_depth = jnp.where(apart == 0, 3.0 * stencil_weights[0], 0.0)
+    for k in range(1, 5):
+        along_depth = along_depth + jnp.where((apart == k) | (apart == -k), stencil_weights[k], 0.0)
+
+    def depth(ref, out):
+        field = ref[pl.ds(H, R), pl.ds(PAD, NX), :].reshape(R * NX, LANES)
+        out[...] = lax.dot_general(
+            field,
+            along_depth,
+            (((1,), (0,)), ((), ())),
+            precision=lax.Precision.HIGHEST,
+            preferred_element_type=jnp.float32,
+        ).reshape(R, NX, LANES)
+
+    def laplace(ref, along, r):
+        summed = along[r]
         for k in range(1, 5):
-            weight = stencil_weights[k]
             around = (ref[H + r + k, pl.ds(PAD, NX), :] + ref[H + r - k, pl.ds(PAD, NX), :]) + (
                 ref[H + r, pl.ds(PAD + k, NX), :] + ref[H + r, pl.ds(PAD - k, NX), :]
             )
-            summed = summed + weight * around
-            summed = summed + jnp.where(lane >= k, weight, 0.0) * pltpu.roll(field, k, 1)
-            summed = summed + jnp.where(lane < LANES - k, weight, 0.0) * pltpu.roll(field, LANES - k, 1)
-        return field, summed
+            summed = summed + stencil_weights[k] * around
+        return summed
 
     def injected(r, amplitude):
         return jnp.where(flat == source - (start_second + r) * LANES, amplitude, 0.0)
 
-    pl.semaphore_wait(
-        barrier, len(peers) + has_lower.astype(jnp.int32) + has_upper.astype(jnp.int32)
-    )
+    def wave_row(t):
+        now, early, later = U.at[t], U.at[t - 1], U.at[t + 1]
+        amplitude = wavelet[0, t - 1]
+
+        def body(r):
+            field = now[centre(r)]
+            second_diff = square[r] * laplace(now, zu, r) + injected(r, amplitude)
+            later[centre(r)] = (2.0 * field - early[centre(r)]) + second_diff
+            term = W[(t, *centre(r))] * second_diff
+            G[r] = term if t == 1 else G[r] + term
+
+        return body
+
+    def adjoint_row(t, last=False):
+        now, early = W.at[t], W.at[t - 1]
+
+        def body(r):
+            value = (2.0 * now[centre(r)] - early[centre(r)]) + (
+                square[r] * laplace(now, zw, r) + received[t - 1, r]
+            )
+            if last:
+                outs[1, pl.ds(r, NX, stride=R), :] = value
+            else:
+                W[(t + 1, *centre(r))] = value
+
+        return body
+
+    pl.semaphore_wait(barrier, count)
     loads[0].wait()
 
     def turn_wave(r):
@@ -225,6 +288,7 @@
 
     over(0, R, turn_adjoint)
     halo_w[1].start()
+    depth(U.at[1], zu)
     loads[2].wait()
     loads[3].wait()
     loads[4].wait()
@@ -235,46 +299,33 @@
         v = turned(4, r)
         speed[r] = v
         square[r] = v * v
-        here = (first * NY + (start_second + r)) * LANES + RDEPTH
-        picks = jnp.where(receiver_cell[...] == here, 1.0, 0.0)
+
+    over(0, R, turn_rest)
+    over(H, R - H, wave_row(1))
+
+    def receive():
+        shape = (R, NX, LANES)
+        here = (
+            lax.broadcasted_iota(jnp.int32, shape, 1) * NY
+            + lax.broadcasted_iota(jnp.int32, shape, 0)
+            + start_second
+        ) * LANES + RDEPTH
+        picks = jnp.where(here == receiver_cell[...].reshape(1, 1, LANES), 1.0, 0.0)
+        picks = picks.astype(jnp.bfloat16).reshape(R * NX, LANES)
+        at_depth = lax.broadcasted_iota(jnp.int32, (LANES, LANES), 0) == RDEPTH
         for t in range(STEPS):
-            sub = lax.broadcasted_iota(jnp.int32, (LANES, LANES), 0)
-            values = jnp.where(sub == RDEPTH, residual[t : t + 1, :], 0.0)
-            received[t, r] = lax.dot_general(
-                picks,
-                values,
-                (((1,), (1,)), ((), ())),
-                precision=lax.Precision.HIGHEST,
-                preferred_element_type=jnp.float32,
-            )
-
-    over(0, R, turn_rest)
-
-    def wave_row(t):
-        now, early, later = U.at[t], U.at[t - 1], U.at[t + 1]
-        amplitude = wavelet[0, t - 1]
-
-        def body(r):
-            field, summed = laplace(now, r)
-            second_diff = square[r] * summed + injected(r, amplitude)
-            later[centre(r)] = (2.0 * field - early[centre(r)]) + second_diff
-            term = W[(t, *centre(r))] * second_diff
-            G[r] = term if t == 1 else G[r] + term
-
-        return body
-
-    def adjoint_row(t, last=False):
-        now, early = W.at[t], W.at[t - 1]
-
-        def body(r):
-            field, summed = laplace(now, r)
-            value = (2.0 * field - early[centre(r)]) + (square[r] * summed + received[t - 1, r])
-            if last:
-                outs[1, pl.ds(r, NX, stride=R), :] = value
-            else:
-                W[(t + 1, *centre(r))] = value
-
-        return body
+            rest, total = jnp.where(at_depth, residual[t], 0.0), None
+            for _ in range(3):
+                part = rest.astype(jnp.bfloat16)
+                rest = rest - part.astype(jnp.float32)
+                picked = lax.dot_general(
+                    picks, part, (((1,), (1,)), ((), ())), preferred_element_type=jnp.float32
+                )
+                total = picked if total is None else total + picked
+            received[t] = total.reshape(shape)
+
+    receive()
+    depth(W.at[1], zw)
 
     class Reduce:
         def __init__(self, which, ref):
@@ -311,9 +362,15 @@
                 device_id_type=MESH,
             )
 
-        def start_x(self):
-            for copy in self.x:
-                copy.start()
+        def start_x(self, part):
+            d = lax.rem(part - x + X, X)
+
+            @pl.when(d > 0)
+            def _():
+                slot = lax.max(d - 1, 0)
+                self.copy(
+                    slot, self.ref.at[pl.ds(part * q, q)], rx.at[self.which, slot], peer_x(d)
+                ).start()
 
         def then_z(self):
             for copy in self.x:
@@ -358,7 +415,8 @@
     reduce_g, reduce_i = Reduce(0, G), Reduce(1, I)
 
     for t in range(1, STEPS):
-        over(H, R - H, wave_row(t))
+        if t > 1:
+            over(H, R - H, wave_row(t))
         halo_u[t].arrive()
         over_edges(wave_row(t))
         halo_u[t + 1].start()
@@ -366,19 +424,27 @@
         halo_w[t].arrive()
         over_edges(adjoint_row(t))
         halo_w[t + 1].start()
+        depth(U.at[t + 1], zu)
+        if t + 1 < STEPS:
+            depth(W.at[t + 1], zw)
 
     def light(r):
         one, two, three = (U[(t, *centre(r))] for t in range(1, 4))
         I[r] = (one * one + two * two) + three * three
 
     over(0, R, light)
-    reduce_i.start_x()
+    for part in range(X):
+        reduce_i.start_x(part)
     over(H, R - H, wave_row(STEPS))
+    for part in range(1, X - 1):
+        reduce_g.start_x(part)
     halo_u[STEPS].arrive()
     over_edges(wave_row(STEPS))
+    for part in (0, X - 1):
+        reduce_g.start_x(part)
     halo_u[STEPS + 1].start()
-    reduce_g.start_x()
     reduce_i.then_z()
+    depth(W.at[STEPS], zw)
     over(H, R - H, adjoint_row(STEPS, last=True))
     halo_w[STEPS].arrive()
     over_edges(adjoint_row(STEPS, last=True))
@@ -386,20 +452,69 @@
     adjoint_store.start()
     reduce_i.then_y()
 
+    depth(U.at[STEPS + 1], zu)
+
+    def before_update(r):
+        L[r] = laplace(U.at[STEPS + 1], zu, r)
+        U[(STEPS + 2, *centre(r))] = (
+            2.0 * U[(STEPS + 1, *centre(r))] - U[(STEPS, *centre(r))]
+        ) + injected(r, wavelet[0, STEPS])
+
+    over(H, R - H, before_update)
+    halo_u[STEPS + 1].arrive()
+    over_edges(before_update)
+    illumination = reduce_i.piece()
     reduce_g.then_z()
-
-    def last_laplace(r):
-        L[r] = laplace(U.at[STEPS + 1], r)[1]
-
-    over(H, R - H, last_laplace)
     reduce_g.then_y()
-    halo_u[STEPS + 1].arrive()
-    over_edges(last_laplace)
-    illumination = reduce_i.piece()
     gradient = reduce_g.piece()
 
-    row = H + x * q + z * h
-    F[pl.ds(row, h), pl.ds(pl.multiple_of(y * c, c), c), :] = gradient / jnp.sqrt(illumination + 1.0)
+    E[pl.ds(H, h), pl.ds(c, c), :] = gradient / jnp.sqrt(illumination + 1.0)
+
+    def index_of(d, e):
+        return (d + reach) * 3 + e + 1
+
+    def to_near(d, e):
+        return pltpu.make_async_remote_copy(
+            src_ref=E.at[pl.ds(H, h), pl.ds(c, c), :],
+            dst_ref=E.at[pl.ds(H - d * h, h), pl.ds(c - e * c, c), :],
+            send_sem=near_send.at[index_of(d, e)],
+            recv_sem=near_recv.at[index_of(-d, -e)],
+            device_id=owner(d, e),
+            device_id_type=MESH,
+        )
+
+    for d, e in near:
+        pl.when(is_near(d, e))(to_near(d, e).start)
+    for d, e in near:
+        pl.when(is_near(d, e))(to_near(-d, -e).wait_recv)
+
+    row = x * q + z * h
+    at_first = y * c - c + lax.broadcasted_iota(jnp.int32, (1, 3 * c, 1), 1)
+    face_first = (at_first >= 0) & (at_first + 1 < NX)
+    face_third = lax.broadcasted_iota(jnp.int32, (1, 1, LANES), 2) < LANES - 1
+
+    def conduct(rise):
+        return rise / (1.0 + rise * rise)
+
+    smoothed = E[...]
+    for turn in range(PASSES):
+        rows = smoothed.shape[0]
+        at_second = (start_second + row - H + turn + 1) + lax.broadcasted_iota(
+            jnp.int32, (rows - 1, 1, 1), 0
+        )
+        face_second = (at_second > 0) & (at_second < NY)
+        second = jnp.where(face_second, conduct(smoothed[1:] - smoothed[:-1]), 0.0)
+        field = smoothed[1:-1]
+        along_first = jnp.where(face_first, conduct(pltpu.roll(field, 3 * c - 1, 1) - field), 0.0)
+        along_third = jnp.where(face_third, conduct(pltpu.roll(field, LANES - 1, 2) - field), 0.0)
+        change = (
+            (along_first - pltpu.roll(along_first, 1, 1))
+            + (second[1:] - second[:-1])
+            + (along_third - pltpu.roll(along_third, 1, 2))
+        )
+        smoothed = field + diffuse_rate * change
+    mine = pl.ds(row, h), pl.ds(pl.multiple_of(y * c, c), c), slice(None)
+    S[mine] = jnp.clip(speed[mine] - step_length * smoothed[:, c : 2 * c], speed_floor, speed_ceiling)
 
     def share(index, part, peer):
         return pltpu.make_async_remote_copy(
@@ -411,105 +526,77 @@
             device_id_type=MESH,
         )
 
-    part_y = F.at[pl.ds(row, h), pl.ds(pl.multiple_of(y * c, c), c), :]
-    shares = [share(X + Z + d - 3, part_y, peer_y(d)) for d in range(1, Y)]
-    for copy in shares:
+    by_y = [share(X + Z + d - 3, S.at[mine], peer_y(d)) for d in range(1, Y)]
+    for copy in by_y:
         copy.start()
-    for copy in shares:
+    for copy in by_y:
         copy.wait_recv()
-    sent = shares
-    part_z = F.at[pl.ds(row, h)]
-    shares = [share(X + d - 2, part_z, peer_z(d)) for d in range(1, Z)]
-    for copy in shares:
+    by_z = [share(X + d - 2, S.at[pl.ds(row, h)], peer_z(d)) for d in range(1, Z)]
+    for copy in by_z:
         copy.start()
-    for copy in shares:
+    for copy in by_z:
         copy.wait_recv()
-    sent = sent + shares
-    part_x = F.at[pl.ds(H + x * q, q)]
-    shares = [share(d - 1, part_x, peer_x(d)) for d in range(1, X)]
-    for copy in shares:
+    by_x = [share(d - 1, S.at[pl.ds(x * q, q)], peer_x(d)) for d in range(1, X)]
+    for copy in by_x:
         copy.start()
-    for copy in shares:
-        copy.wait_recv()
-    sent = sent + shares
-    halo_f.start()
-    halo_f.arrive()
-
-    def conduct(rise):
-        return rise / (1.0 + rise * rise)
-
-    def diffuse(src, last, put):
-        def face(r, rise):
-            at = start_second + (r - H)
-            return jnp.where((at > 0) & (at < NY), conduct(rise), 0.0)
-
-        begin, end = last + 1, R + 2 * H - 1 - last
-
-        def body(r, carry):
-            below, field = carry
-            higher = src[r + 1]
-            above = face(r + 1, higher - field)
-            along_first = jnp.where(first < NX - 1, conduct(pltpu.roll(field, NX - 1, 0) - field), 0.0)
-            along_third = jnp.where(lane < LANES - 1, conduct(pltpu.roll(field, LANES - 1, 1) - field), 0.0)
-            change = (
-                (along_first - pltpu.roll(along_first, 1, 0))
-                + (above - below)
-                + (along_third - pltpu.roll(along_third, 1, 1))
-            )
-            put(r, field + diffuse_rate * change)
-            return above, higher
-
-        field = src[begin]
-        lax.fori_loop(begin, end, body, (face(begin, field - src[begin - 1]), field))
-
-    def into(ref):
-        def put(r, value):
-            ref[r] = value
-
-        return put
-
-    def update(r, value):
-        new_speed = jnp.clip(speed[r - H] - step_length * value, speed_floor, speed_ceiling)
-        outs[2, pl.ds(r - H, NX, stride=R), :] = new_speed
-        square[r - H] = new_speed * new_speed
-
-    diffuse(F, 0, into(FA))
-    diffuse(FA, 1, into(FB))
-    diffuse(FB, 2, into(FA))
-    diffuse(FA, 3, update)
+
+    def final_one(r):
+        new_speed = S[r]
+        outs[2, pl.ds(r, NX, stride=R), :] = new_speed
+        new_square = new_speed * new_speed
+        square[r] = new_square
+        U[(STEPS + 2, *centre(r))] = U[(STEPS + 2, *centre(r))] + new_square * L[r]
+
+    def final_two(r):
+        outs[0, pl.ds(r, NX, stride=R), :] = (
+            2.0 * U[(STEPS + 2, *centre(r))] - U[(STEPS + 1, *centre(r))]
+        ) + (square[r] * laplace(U.at[STEPS + 2], zu, r) + injected(r, wavelet[0, STEPS + 1]))
+
+    def part_of_first(part):
+        d = lax.rem(x - part + X, X)
+
+        @pl.when(d > 0)
+        def _():
+            share(lax.max(d - 1, 0), S.at[pl.ds(part * q, q)], peer_x(d)).wait_recv()
+
+        over(part * q, part * q + q, final_one)
+
+    for part in (0, X - 1):
+        part_of_first(part)
+    halo_u[STEPS + 2].start()
+    for part in range(1, X - 1):
+        part_of_first(part)
     speed_store = pltpu.make_async_copy(outs.at[2], speed_out, out_sem.at[2])
     speed_store.start()
-
-    def final_one(r):
-        value = (2.0 * U[(STEPS + 1, *centre(r))] - U[(STEPS, *centre(r))]) + (
-            square[r] * L[r] + injected(r, wavelet[0, STEPS])
-        )
-        U[(STEPS + 2, *centre(r))] = value
-
-    def final_two(r):
-        field, summed = laplace(U.at[STEPS + 2], r)
-        outs[0, pl.ds(r, NX, stride=R), :] = (2.0 * field - U[(STEPS + 1, *centre(r))]) + (
-            square[r] * summed + injected(r, wavelet[0, STEPS + 1])
-        )
-
-    over_edges(final_one)
-    halo_u[STEPS + 2].start()
-    over(H, R - H, final_one)
+    depth(U.at[STEPS + 2], zu)
     over(H, R - H, final_two)
     halo_u[STEPS + 2].arrive()
     over_edges(final_two)
     wave_store = pltpu.make_async_copy(outs.at[0], wave_out, out_sem.at[0])
     wave_store.start()
 
-    for halo in (*halo_u.values(), *halo_w.values(), halo_f):
+    for halo in (*halo_u.values(), *halo_w.values()):
         halo.leave()
     reduce_g.leave()
     reduce_i.leave()
-    for copy in sent:
+    for d, e in near:
+        pl.when(is_near(d, e))(to_near(d, e).wait_send)
+    for copy in by_y + by_z + by_x:
         copy.wait_send()
     adjoint_store.wait()
     speed_store.wait()
     wave_store.wait()
+
+
+def hand_over(wave, adjoint, speed, wave_out, adjoint_out, speed_out, sem):
+    copies = [
+        pltpu.make_async_copy(src, dst, sem.at[i])
+        for i, (src, dst) in enumerate(((wave, wave_out), (adjoint, adjoint_out), (speed, speed_out)))
+    ]
+    for copy in copies:
+        copy.start()
+    for copy in copies:
+        copy.wait()
 
 
 def local(
@@ -532,8 +619,8 @@
     flat = (NX * R, D)
     padded = (R + 2 * H, NX + 2 * PAD, D)
     plain = (R, NX, D)
-    around = (R + 2 * H, NX, D)
     n_rs = X + Y + Z - 3
+    n_near = 3 * (2 * -(-H // h) + 1)
     vmem, smem, anywhere = (
         pl.BlockSpec(memory_space=pltpu.VMEM),
         pl.BlockSpec(memory_space=pltpu.SMEM),
@@ -559,19 +646,22 @@
             pltpu.VMEM((2, max(Y - 1, 1), h, c, D), f32),
             pltpu.VMEM((2, q, NX, D), f32),
             pltpu.VMEM((2, h, NX, D), f32),
-            pltpu.VMEM(around, f32),
-            pltpu.VMEM(around, f32),
-            pltpu.VMEM(around, f32),
+            pltpu.VMEM((h + 2 * H, 3 * c, D), f32),
+            pltpu.VMEM(plain, f32),
+            pltpu.VMEM(plain, f32),
+            pltpu.VMEM(plain, f32),
             pltpu.VMEM(plain, f32),
             pltpu.VMEM((3, *flat), f32),
             pltpu.SemaphoreType.DMA((5,)),
             pltpu.SemaphoreType.DMA((3,)),
-            pltpu.SemaphoreType.DMA((9, 2)),
-            pltpu.SemaphoreType.DMA((9, 2)),
+            pltpu.SemaphoreType.DMA((8, 2)),
+            pltpu.SemaphoreType.DMA((8, 2)),
             pltpu.SemaphoreType.DMA((2, n_rs)),
             pltpu.SemaphoreType.DMA((2, n_rs)),
             pltpu.SemaphoreType.DMA((n_rs,)),
             pltpu.SemaphoreType.DMA((n_rs,)),
+            pltpu.SemaphoreType.DMA((n_near,)),
+            pltpu.SemaphoreType.DMA((n_near,)),
         ],
         compiler_params=pltpu.CompilerParams(
             collective_id=0, has_side_effects=True, vmem_limit_bytes=56 * 1024 * 1024
@@ -580,13 +670,20 @@
         source_cell,
         wavelet,
         receiver_cell,
-        residual.reshape(residual.shape[1:]),
+        residual.transpose(1, 0, 2),
         wave_prev.reshape(flat),
         wave_now.reshape(flat),
         adjoint_prev.reshape(flat),
         adjoint_now.reshape(flat),
         velocity.reshape(flat),
     )
+    wave_out, adjoint_out, speed_out = pl.pallas_call(
+        hand_over,
+        out_shape=(out, out, out),
+        in_specs=[anywhere] * 3,
+        out_specs=(anywhere,) * 3,
+        scratch_shapes=[pltpu.SemaphoreType.DMA((3,))],
+    )(wave_out, adjoint_out, speed_out)
     field = (1, NX, R, D)
     return wave_out.reshape(field), adjoint_out.reshape(field), speed_out.reshape(field[1:])
 

time: 95.1 us -> 133 us (1.40); the launches traced: 94.9 us -> 131 us
  Pallas kernels: 88.4 us -> 130 us
  local copies, waits for them, and re-layouts: 5.2 us -> 0 us
    pallas_call x0 -> x1, Pallas kernels: none -> 48.8 us  [local(): pl.pallas_call(hand_over, out_shape=(out, out, out), in_specs=[anywhere]...]
    pallas_call x1, Pallas kernels: 88.4 us -> 81.2 us  [local(): pl.pallas_call(functools.partial(kernel, (X, Z, Y, boxes, NX, R)), out_sh...]
    unnamed x10 -> x0, local copies, waits for them, and re-layouts: 5.2 us -> none
where the time goes in v2:
time: 133 us; the launch traced here: 131 us
  Pallas kernels  130 us (98%)
    pallas_call x1, Pallas kernels, local(): pl.pallas_call(functools.partial(kernel, (X, Z, Y, boxes, NX, R)), out_sh...  81.2 us
    pallas_call x1, Pallas kernels, local(): pl.pallas_call(hand_over, out_shape=(out, out, out), in_specs=[anywhere]...  48.8 us

profile of v2, /device:TPU:1, one launch (start us, length us, event | category | flops | bytes accessed | tf_op | source)
XLA Modules:
  0.0 131.2 jit_solution(4796729293226754121)
XLA Ops:
  1.3 81.2 %shard_map.112 = (f32[1024,128]{1,0:T(8,128)}, f32[1024,128]{1,0:T(8,128)}, f32[1024,128]{1,0:T(8,128)}) custom-call(s32[1]{0:T(128)S(6)} %copy.12.source_cell, f32[1,5]{1,0:T(1,128)} %wavelet.1, s32[1,128]{1,0:T(1,128)} %receiver_cell.1, f32[3,1,128]{2,1,0:T(1,128)} %bitcast.14, f32[1024,128]{1,0:T(8,128)} %bitcast.9, f32[1024,128]{1,0:T(8,128)} %bitcast.10, ...), custom_call_target="tpu_custom_call" | custom-call | tf_op jit(solution)/shard_map/pallas_call | solution.py:630
  82.5 48.8 %shard_map.113 = (f32[1024,128]{1,0:T(8,128)}, f32[1024,128]{1,0:T(8,128)}, f32[1024,128]{1,0:T(8,128)}) custom-call(f32[1024,128]{1,0:T(8,128)} %get-tuple-element.9.wave, f32[1024,128]{1,0:T(8,128)} %get-tuple-element.10.adjoint, f32[1024,128]{1,0:T(8,128)} %get-tuple-element.11.speed), custom_call_target="tpu_custom_call" | custom-call | tf_op jit(solution)/shard_map/pallas_call | solution.py:680

commit v3 on v2

--- a/solution.py
+++ b/solution.py
@@ -46,18 +46,14 @@
     G,
     I,
     rx,
-    rz,
-    ry,
+    rp,
     sx,
-    sz,
     E,
     S,
     L,
     zu,
     zw,
-    outs,
     in_sem,
-    out_sem,
     halo_send,
     halo_recv,
     rs_send,
@@ -80,11 +76,10 @@
     def peer_x(d):
         return (lax.rem(x + d, X) * Z + z) * Y + y
 
-    def peer_z(d):
-        return (x * Z + lax.rem(z + d, Z)) * Y + y
-
-    def peer_y(d):
-        return (x * Z + z) * Y + lax.rem(y + d, Y)
+    def peer_zy(d, e):
+        return (x * Z + lax.rem(z + d, Z)) * Y + lax.rem(y + e, Y)
+
+    plane = [(d, e) for d in range(Z) for e in range(Y) if (d, e) != (0, 0)]
 
     pieces = X * Z
     place = box * pieces + x * Z + z
@@ -112,11 +107,7 @@
         load.start()
 
     barrier = pltpu.get_barrier_semaphore()
-    peers = (
-        [peer_x(d) for d in range(1, X)]
-        + [peer_z(d) for d in range(1, Z)]
-        + [peer_y(d) for d in range(1, Y)]
-    )
+    peers = [peer_x(d) for d in range(1, X)] + [peer_zy(d, e) for d, e in plane]
     for peer in peers:
         pl.semaphore_signal(barrier, inc=1, device_id={"shot": peer}, device_id_type=MESH)
 
@@ -267,7 +258,7 @@
                 square[r] * laplace(now, zw, r) + received[t - 1, r]
             )
             if last:
-                outs[1, pl.ds(r, NX, stride=R), :] = value
+                adjoint_out[pl.ds(r, NX, stride=R), :] = value
             else:
                 W[(t + 1, *centre(r))] = value
 
@@ -287,7 +278,6 @@
         W[(1, *centre(r))] = turned(1, r)
 
     over(0, R, turn_adjoint)
-    halo_w[1].start()
     depth(U.at[1], zu)
     loads[2].wait()
     loads[3].wait()
@@ -303,7 +293,7 @@
     over(0, R, turn_rest)
     over(H, R - H, wave_row(1))
 
-    def receive():
+    def receive(t):
         shape = (R, NX, LANES)
         here = (
             lax.broadcasted_iota(jnp.int32, shape, 1) * NY
@@ -313,19 +303,21 @@
         picks = jnp.where(here == receiver_cell[...].reshape(1, 1, LANES), 1.0, 0.0)
         picks = picks.astype(jnp.bfloat16).reshape(R * NX, LANES)
         at_depth = lax.broadcasted_iota(jnp.int32, (LANES, LANES), 0) == RDEPTH
-        for t in range(STEPS):
-            rest, total = jnp.where(at_depth, residual[t], 0.0), None
-            for _ in range(3):
-                part = rest.astype(jnp.bfloat16)
-                rest = rest - part.astype(jnp.float32)
-                picked = lax.dot_general(
-                    picks, part, (((1,), (1,)), ((), ())), preferred_element_type=jnp.float32
-                )
-                total = picked if total is None else total + picked
-            received[t] = total.reshape(shape)
-
-    receive()
+        rest, total = jnp.where(at_depth, residual[t - 1], 0.0), None
+        for _ in range(3):
+            part = rest.astype(jnp.bfloat16)
+            rest = rest - part.astype(jnp.float32)
+            picked = lax.dot_general(
+                picks, part, (((1,), (1,)), ((), ())), preferred_element_type=jnp.float32
+            )
+            total = picked if total is None else total + picked
+        received[t - 1] = total.reshape(shape)
+
+    receive(1)
+    halo_u[1].leave()
+    halo_w[1].start()
     depth(W.at[1], zw)
+
 
     class Reduce:
         def __init__(self, which, ref):
@@ -334,23 +326,20 @@
             for d in range(1, X):
                 target = lax.rem(x + d, X)
                 self.x.append(self.copy(d - 1, ref.at[pl.ds(target * q, q)], rx.at[which, d - 1], peer_x(d)))
-            self.z = []
-            for d in range(1, Z):
-                target = lax.rem(z + d, Z)
-                self.z.append(
-                    self.copy(X + d - 2, sx.at[which, pl.ds(target * h, h)], rz.at[which, d - 1], peer_z(d))
+            self.p = [
+                self.copy(
+                    X - 1 + i,
+                    sx.at[
+                        which,
+                        pl.ds(lax.rem(z + d, Z) * h, h),
+                        pl.ds(pl.multiple_of(lax.rem(y + e, Y) * c, c), c),
+                        :,
+                    ],
+                    rp.at[which, i],
+                    peer_zy(d, e),
                 )
-            self.y = []
-            for d in range(1, Y):
-                target = lax.rem(y + d, Y)
-                self.y.append(
-                    self.copy(
-                        X + Z + d - 3,
-                        sz.at[which, :, pl.ds(pl.multiple_of(target * c, c), c), :],
-                        ry.at[which, d - 1],
-                        peer_y(d),
-                    )
-                )
+                for i, (d, e) in enumerate(plane)
+            ]
 
         def copy(self, index, src, dst, peer):
             return pltpu.make_async_remote_copy(
@@ -372,7 +361,7 @@
                     slot, self.ref.at[pl.ds(part * q, q)], rx.at[self.which, slot], peer_x(d)
                 ).start()
 
-        def then_z(self):
+        def then_plane(self):
             for copy in self.x:
                 copy.wait_recv()
 
@@ -383,50 +372,42 @@
                 sx[self.which, r] = total
 
             over(0, q, add)
-            for copy in self.z:
+            for copy in self.p:
                 copy.start()
 
-        def then_y(self):
-            for copy in self.z:
+        def piece(self):
+            for copy in self.p:
                 copy.wait_recv()
-
-            def add(r):
-                total = sx[self.which, z * h + r]
-                for d in range(1, Z):
-                    total = total + rz[self.which, d - 1, r]
-                sz[self.which, r] = total
-
-            over(0, h, add)
-            for copy in self.y:
-                copy.start()
-
-        def piece(self):
-            for copy in self.y:
-                copy.wait_recv()
-            total = sz[self.which, :, pl.ds(pl.multiple_of(y * c, c), c), :]
-            for d in range(1, Y):
-                total = total + ry[self.which, d - 1]
+            total = sx[self.which, pl.ds(z * h, h), pl.ds(pl.multiple_of(y * c, c), c), :]
+            for i in range(len(self.p)):
+                total = total + rp[self.which, i]
             return total
 
         def leave(self):
-            for copy in self.x + self.z + self.y:
+            for copy in self.x + self.p:
                 copy.wait_send()
 
     reduce_g, reduce_i = Reduce(0, G), Reduce(1, I)
 
-    for t in range(1, STEPS):
-        if t > 1:
-            over(H, R - H, wave_row(t))
-        halo_u[t].arrive()
-        over_edges(wave_row(t))
-        halo_u[t + 1].start()
-        over(H, R - H, adjoint_row(t))
-        halo_w[t].arrive()
-        over_edges(adjoint_row(t))
-        halo_w[t + 1].start()
-        depth(U.at[t + 1], zu)
-        if t + 1 < STEPS:
-            depth(W.at[t + 1], zw)
+    halo_u[1].arrive()
+    over_edges(wave_row(1))
+    halo_u[2].start()
+    over(H, R - H, adjoint_row(1))
+    receive(2)
+    halo_w[1].arrive()
+    over_edges(adjoint_row(1))
+    halo_w[2].start()
+    depth(U.at[2], zu)
+    over(H, R - H, wave_row(2))
+    halo_u[2].arrive()
+    over_edges(wave_row(2))
+    halo_u[3].start()
+    depth(W.at[2], zw)
+    over(H, R - H, adjoint_row(2))
+    depth(U.at[3], zu)
+    over(H, R - H, wave_row(3))
+    for part in range(1, X - 1):
+        reduce_g.start_x(part)
 
     def light(r):
         one, two, three = (U[(t, *centre(r))] for t in range(1, 4))
@@ -435,22 +416,18 @@
     over(0, R, light)
     for part in range(X):
         reduce_i.start_x(part)
-    over(H, R - H, wave_row(STEPS))
-    for part in range(1, X - 1):
-        reduce_g.start_x(part)
-    halo_u[STEPS].arrive()
-    over_edges(wave_row(STEPS))
+    receive(3)
+    halo_w[2].arrive()
+    over_edges(adjoint_row(2))
+    halo_u[3].arrive()
+    over_edges(wave_row(3))
     for part in (0, X - 1):
         reduce_g.start_x(part)
-    halo_u[STEPS + 1].start()
-    reduce_i.then_z()
-    depth(W.at[STEPS], zw)
-    over(H, R - H, adjoint_row(STEPS, last=True))
-    halo_w[STEPS].arrive()
-    over_edges(adjoint_row(STEPS, last=True))
-    adjoint_store = pltpu.make_async_copy(outs.at[1], adjoint_out, out_sem.at[1])
-    adjoint_store.start()
-    reduce_i.then_y()
+    halo_u[4].start()
+    halo_w[3].start()
+    reduce_i.then_plane()
+    depth(W.at[3], zw)
+    over(H, R - H, adjoint_row(3, last=True))
 
     depth(U.at[STEPS + 1], zu)
 
@@ -461,11 +438,8 @@
         ) + injected(r, wavelet[0, STEPS])
 
     over(H, R - H, before_update)
-    halo_u[STEPS + 1].arrive()
-    over_edges(before_update)
+    reduce_g.then_plane()
     illumination = reduce_i.piece()
-    reduce_g.then_z()
-    reduce_g.then_y()
     gradient = reduce_g.piece()
 
     E[pl.ds(H, h), pl.ds(c, c), :] = gradient / jnp.sqrt(illumination + 1.0)
@@ -485,6 +459,8 @@
 
     for d, e in near:
         pl.when(is_near(d, e))(to_near(d, e).start)
+    halo_u[STEPS + 1].arrive()
+    over_edges(before_update)
     for d, e in near:
         pl.when(is_near(d, e))(to_near(-d, -e).wait_recv)
 
@@ -526,29 +502,33 @@
             device_id_type=MESH,
         )
 
-    by_y = [share(X + Z + d - 3, S.at[mine], peer_y(d)) for d in range(1, Y)]
-    for copy in by_y:
+    by_plane = [
+        share(X - 1 + i, S.at[mine], peer_zy(d, e)) for i, (d, e) in enumerate(plane)
+    ]
+    for copy in by_plane:
         copy.start()
-    for copy in by_y:
-        copy.wait_recv()
-    by_z = [share(X + d - 2, S.at[pl.ds(row, h)], peer_z(d)) for d in range(1, Z)]
-    for copy in by_z:
-        copy.start()
-    for copy in by_z:
+    halo_w[3].arrive()
+    over_edges(adjoint_row(3, last=True))
+    for copy in by_plane:
         copy.wait_recv()
     by_x = [share(d - 1, S.at[pl.ds(x * q, q)], peer_x(d)) for d in range(1, X)]
-    for copy in by_x:
-        copy.start()
+
+    def send_part():
+        for copy in by_x:
+            copy.start()
+
+    inner = (x > 0) & (x < X - 1)
+    pl.when(jnp.logical_not(inner))(send_part)
 
     def final_one(r):
         new_speed = S[r]
-        outs[2, pl.ds(r, NX, stride=R), :] = new_speed
+        speed_out[pl.ds(r, NX, stride=R), :] = new_speed
         new_square = new_speed * new_speed
         square[r] = new_square
         U[(STEPS + 2, *centre(r))] = U[(STEPS + 2, *centre(r))] + new_square * L[r]
 
     def final_two(r):
-        outs[0, pl.ds(r, NX, stride=R), :] = (
+        wave_out[pl.ds(r, NX, stride=R), :] = (
             2.0 * U[(STEPS + 2, *centre(r))] - U[(STEPS + 1, *centre(r))]
         ) + (square[r] * laplace(U.at[STEPS + 2], zu, r) + injected(r, wavelet[0, STEPS + 1]))
 
@@ -564,28 +544,22 @@
     for part in (0, X - 1):
         part_of_first(part)
     halo_u[STEPS + 2].start()
+    pl.when(inner)(send_part)
     for part in range(1, X - 1):
         part_of_first(part)
-    speed_store = pltpu.make_async_copy(outs.at[2], speed_out, out_sem.at[2])
-    speed_store.start()
     depth(U.at[STEPS + 2], zu)
     over(H, R - H, final_two)
     halo_u[STEPS + 2].arrive()
     over_edges(final_two)
-    wave_store = pltpu.make_async_copy(outs.at[0], wave_out, out_sem.at[0])
-    wave_store.start()
-
-    for halo in (*halo_u.values(), *halo_w.values()):
+
+    for halo in (*list(halo_u.values())[1:], *halo_w.values()):
         halo.leave()
     reduce_g.leave()
     reduce_i.leave()
     for d, e in near:
         pl.when(is_near(d, e))(to_near(d, e).wait_send)
-    for copy in by_y + by_z + by_x:
+    for copy in by_plane + by_x:
         copy.wait_send()
-    adjoint_store.wait()
-    speed_store.wait()
-    wave_store.wait()
 
 
 def hand_over(wave, adjoint, speed, wave_out, adjoint_out, speed_out, sem):
@@ -619,7 +593,7 @@
     flat = (NX * R, D)
     padded = (R + 2 * H, NX + 2 * PAD, D)
     plain = (R, NX, D)
-    n_rs = X + Y + Z - 3
+    n_rs = X + Z * Y - 2
     n_near = 3 * (2 * -(-H // h) + 1)
     vmem, smem, anywhere = (
         pl.BlockSpec(memory_space=pltpu.VMEM),
@@ -627,11 +601,12 @@
         pl.BlockSpec(memory_space=pl.ANY),
     )
     out = jax.ShapeDtypeStruct(flat, f32)
+    kept = pltpu.VMEM(flat, f32)
     wave_out, adjoint_out, speed_out = pl.pallas_call(
         functools.partial(kernel, (X, Z, Y, boxes, NX, R)),
-        out_shape=(out, out, out),
+        out_shape=(kept, kept, kept),
         in_specs=[smem, smem, vmem, vmem] + [anywhere] * 5,
-        out_specs=(anywhere, anywhere, anywhere),
+        out_specs=(vmem, vmem, vmem),
         scratch_shapes=[
             pltpu.VMEM((5, *flat), f32),
             pltpu.VMEM((6, *padded), f32),
@@ -642,18 +617,14 @@
             pltpu.VMEM(plain, f32),
             pltpu.VMEM(plain, f32),
             pltpu.VMEM((2, max(X - 1, 1), q, NX, D), f32),
-            pltpu.VMEM((2, max(Z - 1, 1), h, NX, D), f32),
-            pltpu.VMEM((2, max(Y - 1, 1), h, c, D), f32),
+            pltpu.VMEM((2, Z * Y - 1, h, c, D), f32),
             pltpu.VMEM((2, q, NX, D), f32),
-            pltpu.VMEM((2, h, NX, D), f32),
             pltpu.VMEM((h + 2 * H, 3 * c, D), f32),
             pltpu.VMEM(plain, f32),
             pltpu.VMEM(plain, f32),
             pltpu.VMEM(plain, f32),
             pltpu.VMEM(plain, f32),
-            pltpu.VMEM((3, *flat), f32),
             pltpu.SemaphoreType.DMA((5,)),
-            pltpu.SemaphoreType.DMA((3,)),
             pltpu.SemaphoreType.DMA((8, 2)),
             pltpu.SemaphoreType.DMA((8, 2)),
             pltpu.SemaphoreType.DMA((2, n_rs)),
@@ -680,10 +651,10 @@
     wave_out, adjoint_out, speed_out = pl.pallas_call(
         hand_over,
         out_shape=(out, out, out),
-        in_specs=[anywhere] * 3,
+        in_specs=[vmem] * 3,
         out_specs=(anywhere,) * 3,
         scratch_shapes=[pltpu.SemaphoreType.DMA((3,))],
-    )(wave_out, adjoint_out, speed_out)
+    )(*(pltpu.with_memory_space_constraint(a, pltpu.VMEM) for a in (wave_out, adjoint_out, speed_out)))
     field = (1, NX, R, D)
     return wave_out.reshape(field), adjoint_out.reshape(field), speed_out.reshape(field[1:])
 

time: 133 us -> 79.3 us (0.60)
  Pallas kernels: 130 us -> 77.5 us
    pallas_call x1, Pallas kernels: 48.8 us -> 1.17 us  [local(): pl.pallas_call(hand_over, out_shape=(out, out, out), in_specs=[vmem] * 3,...]
    pallas_call x1, Pallas kernels: 81.2 us -> 76.3 us  [local(): pl.pallas_call(functools.partial(kernel, (X, Z, Y, boxes, NX, R)), out_sh...]
where the time goes in v3:
time: 79.3 us; the launch traced here: 78.8 us
  Pallas kernels  77.5 us (98%)
  between operations  1.29 us (2%)
    pallas_call x1, Pallas kernels, local(): pl.pallas_call(functools.partial(kernel, (X, Z, Y, boxes, NX, R)), out_sh...  76.3 us

profile of v3, /device:TPU:1, one launch (start us, length us, event | category | flops | bytes accessed | tf_op | source)
XLA Modules:
  0.0 78.8 jit_solution(18353032514458113969)
XLA Ops:
  1.3 76.3 %shard_map.112 = (f32[1024,128]{1,0:T(8,128)S(1)}, f32[1024,128]{1,0:T(8,128)S(1)}, f32[1024,128]{1,0:T(8,128)S(1)}) custom-call(s32[1]{0:T(128)S(6)} %copy.12.source_cell, f32[1,5]{1,0:T(1,128)} %wavelet.1, s32[1,128]{1,0:T(1,128)} %receiver_cell.1, f32[3,1,128]{2,1,0:T(1,128)} %bitcast.14, f32[1024,128]{1,0:T(8,128)} %bitcast.9, f32[1024,128]{1,0:T(8,128)} %bitcast.10, ...), custom_call_target="tpu_custom_call" | custom-call | tf_op jit(solution)/shard_map/pallas_call | solution.py:605
  77.6 1.2 %shard_map.113 = (f32[1024,128]{1,0:T(8,128)}, f32[1024,128]{1,0:T(8,128)}, f32[1024,128]{1,0:T(8,128)}) custom-call(f32[1024,128]{1,0:T(8,128)S(1)} %get-tuple-element.9.wave, f32[1024,128]{1,0:T(8,128)S(1)} %get-tuple-element.10.adjoint, f32[1024,128]{1,0:T(8,128)S(1)} %get-tuple-element.11.speed), custom_call_target="tpu_custom_call" | custom-call | tf_op jit(solution)/shard_map/pallas_call | solution.py:651

commit v4 on v3

--- a/solution.py
+++ b/solution.py
@@ -65,7 +65,7 @@
 ):
     X, Z, Y, boxes, NX, R = sizes
     NY = R * boxes
-    q, h, c = R // X, R // (X * Z), NX // Y
+    h, c = R // (X * Z), NX // Y
     shot, box = lax.axis_index("shot"), lax.axis_index("box")
     x = lax.div(shot, Z * Y)
     z = lax.rem(lax.div(shot, Y), Z)
@@ -79,10 +79,22 @@
     def peer_zy(d, e):
         return (x * Z + lax.rem(z + d, Z)) * Y + lax.rem(y + e, Y)
 
+    at_edge = (1, 7, 0, 6)
+    in_middle = (2, 3, 4, 5)
+
+    def chosen(index, table):
+        value = table[0]
+        for i in range(1, len(table)):
+            value = jnp.where(index == i, table[i], value)
+        return value
+
+    def pair_of(x, z):
+        return jnp.where(z == 0, chosen(x, at_edge), chosen(x, in_middle))
+
     plane = [(d, e) for d in range(Z) for e in range(Y) if (d, e) != (0, 0)]
 
     pieces = X * Z
-    place = box * pieces + x * Z + z
+    place = box * pieces + pair_of(x, z)
     reach = -(-H // h)
     beside = [e for e in (-1, 0, 1) if Y > 1 or e == 0]
     near = [(d, e) for d in range(-reach, reach + 1) for e in beside if (d, e) != (0, 0)]
@@ -92,8 +104,11 @@
 
     def owner(d, e):
         other = lax.clamp(0, place + d, boxes * pieces - 1)
+        pair = lax.rem(other, pieces)
+        to_x = chosen(pair, tuple((at_edge + in_middle).index(p) % X for p in range(pieces)))
+        to_z = chosen(pair, tuple((at_edge + in_middle).index(p) // X for p in range(pieces)))
         return {
-            "shot": lax.rem(other, pieces) * Y + lax.clamp(0, y + e, Y - 1),
+            "shot": (to_x * Z + to_z) * Y + lax.clamp(0, y + e, Y - 1),
             "box": lax.div(other, pieces),
         }
 
@@ -322,22 +337,15 @@
     class Reduce:
         def __init__(self, which, ref):
             self.ref, self.which = ref, which
-            self.x = []
-            for d in range(1, X):
-                target = lax.rem(x + d, X)
-                self.x.append(self.copy(d - 1, ref.at[pl.ds(target * q, q)], rx.at[which, d - 1], peer_x(d)))
+            self.x = [
+                [
+                    self.copy(k * (X - 1) + d - 1, ref.at[pl.ds(0, h)], rx.at[which, k, d - 1], peer_x(d))
+                    for d in range(1, X)
+                ]
+                for k in range(Z)
+            ]
             self.p = [
-                self.copy(
-                    X - 1 + i,
-                    sx.at[
-                        which,
-                        pl.ds(lax.rem(z + d, Z) * h, h),
-                        pl.ds(pl.multiple_of(lax.rem(y + e, Y) * c, c), c),
-                        :,
-                    ],
-                    rp.at[which, i],
-                    peer_zy(d, e),
-                )
+                self.copy(Z * (X - 1) + i, ref.at[pl.ds(0, h), pl.ds(0, c), :], rp.at[which, i], peer_zy(d, e))
                 for i, (d, e) in enumerate(plane)
             ]
 
@@ -351,29 +359,43 @@
                 device_id_type=MESH,
             )
 
-        def start_x(self, part):
-            d = lax.rem(part - x + X, X)
-
-            @pl.when(d > 0)
-            def _():
+        def start_x(self, k):
+            for to in range(X):
+                d = lax.rem(to - x + X, X)
                 slot = lax.max(d - 1, 0)
-                self.copy(
-                    slot, self.ref.at[pl.ds(part * q, q)], rx.at[self.which, slot], peer_x(d)
-                ).start()
-
-        def then_plane(self):
-            for copy in self.x:
+                begin = h * (at_edge, in_middle)[k][to]
+                copy = self.copy(
+                    k * (X - 1) + slot, self.ref.at[pl.ds(begin, h)], rx.at[self.which, k, slot], peer_x(d)
+                )
+                pl.when(d > 0)(copy.start)
+
+        def then_plane(self, k):
+            for copy in self.x[k]:
                 copy.wait_recv()
-
-            def add(r):
-                total = self.ref[x * q + r]
+            begin = h * chosen(x, (at_edge, in_middle)[k])
+            for r in range(h):
+                total = self.ref[begin + r]
                 for d in range(1, X):
-                    total = total + rx[self.which, d - 1, r]
-                sx[self.which, r] = total
-
-            over(0, q, add)
-            for copy in self.p:
-                copy.start()
+                    total = total + rx[self.which, k, d - 1, r]
+                sx[self.which, k * h + r] = total
+            d = lax.rem(k - z + Z, Z)
+            for e in range(Y):
+                slot = d * Y + e - 1 if e > 0 else lax.max(d * Y - 1, 0)
+                copy = self.copy(
+                    Z * (X - 1) + slot,
+                    sx.at[
+                        self.which,
+                        pl.ds(k * h, h),
+                        pl.ds(pl.multiple_of(lax.rem(y + e, Y) * c, c), c),
+                        :,
+                    ],
+                    rp.at[self.which, slot],
+                    peer_zy(d, e),
+                )
+                if e > 0:
+                    copy.start()
+                else:
+                    pl.when(d > 0)(copy.start)
 
         def piece(self):
             for copy in self.p:
@@ -384,7 +406,7 @@
             return total
 
         def leave(self):
-            for copy in self.x + self.p:
+            for copy in sum(self.x, []) + self.p:
                 copy.wait_send()
 
     reduce_g, reduce_i = Reduce(0, G), Reduce(1, I)
@@ -406,26 +428,26 @@
     over(H, R - H, adjoint_row(2))
     depth(U.at[3], zu)
     over(H, R - H, wave_row(3))
-    for part in range(1, X - 1):
-        reduce_g.start_x(part)
+    reduce_g.start_x(1)
 
     def light(r):
         one, two, three = (U[(t, *centre(r))] for t in range(1, 4))
         I[r] = (one * one + two * two) + three * three
 
     over(0, R, light)
-    for part in range(X):
-        reduce_i.start_x(part)
+    reduce_i.start_x(1)
+    reduce_i.start_x(0)
     receive(3)
     halo_w[2].arrive()
     over_edges(adjoint_row(2))
     halo_u[3].arrive()
     over_edges(wave_row(3))
-    for part in (0, X - 1):
-        reduce_g.start_x(part)
+    reduce_g.start_x(0)
     halo_u[4].start()
+    reduce_g.then_plane(1)
     halo_w[3].start()
-    reduce_i.then_plane()
+    reduce_i.then_plane(1)
+    reduce_i.then_plane(0)
     depth(W.at[3], zw)
     over(H, R - H, adjoint_row(3, last=True))
 
@@ -438,7 +460,7 @@
         ) + injected(r, wavelet[0, STEPS])
 
     over(H, R - H, before_update)
-    reduce_g.then_plane()
+    reduce_g.then_plane(0)
     illumination = reduce_i.piece()
     gradient = reduce_g.piece()
 
@@ -464,7 +486,7 @@
     for d, e in near:
         pl.when(is_near(d, e))(to_near(-d, -e).wait_recv)
 
-    row = x * q + z * h
+    row = h * pair_of(x, z)
     at_first = y * c - c + lax.broadcasted_iota(jnp.int32, (1, 3 * c, 1), 1)
     face_first = (at_first >= 0) & (at_first + 1 < NX)
     face_third = lax.broadcasted_iota(jnp.int32, (1, 1, LANES), 2) < LANES - 1
@@ -502,23 +524,27 @@
             device_id_type=MESH,
         )
 
+    first_slot = Z * (X - 1)
     by_plane = [
-        share(X - 1 + i, S.at[mine], peer_zy(d, e)) for i, (d, e) in enumerate(plane)
+        share(first_slot + i, S.at[mine], peer_zy(d, e)) for i, (d, e) in enumerate(plane)
     ]
     for copy in by_plane:
         copy.start()
     halo_w[3].arrive()
     over_edges(adjoint_row(3, last=True))
-    for copy in by_plane:
-        copy.wait_recv()
-    by_x = [share(d - 1, S.at[pl.ds(x * q, q)], peer_x(d)) for d in range(1, X)]
-
-    def send_part():
-        for copy in by_x:
+    by_x = []
+    for k in range(Z):
+        d = lax.rem(z - k + Z, Z)
+        for e in range(Y):
+            slot = first_slot + (d * Y + e - 1 if e > 0 else lax.max(d * Y - 1, 0))
+            if e > 0:
+                share(slot, S.at[mine], peer_zy(d, e)).wait_recv()
+            else:
+                pl.when(d > 0)(share(slot, S.at[mine], peer_zy(d, e)).wait_recv)
+        part = S.at[pl.ds(h * chosen(x, (at_edge, in_middle)[k]), h)]
+        by_x.append([share(k * (X - 1) + d - 1, part, peer_x(d)) for d in range(1, X)])
+        for copy in by_x[k]:
             copy.start()
-
-    inner = (x > 0) & (x < X - 1)
-    pl.when(jnp.logical_not(inner))(send_part)
 
     def final_one(r):
         new_speed = S[r]
@@ -532,21 +558,13 @@
             2.0 * U[(STEPS + 2, *centre(r))] - U[(STEPS + 1, *centre(r))]
         ) + (square[r] * laplace(U.at[STEPS + 2], zu, r) + injected(r, wavelet[0, STEPS + 1]))
 
-    def part_of_first(part):
-        d = lax.rem(x - part + X, X)
-
-        @pl.when(d > 0)
-        def _():
-            share(lax.max(d - 1, 0), S.at[pl.ds(part * q, q)], peer_x(d)).wait_recv()
-
-        over(part * q, part * q + q, final_one)
-
-    for part in (0, X - 1):
-        part_of_first(part)
+    for copy in by_x[0]:
+        copy.wait_recv()
+    over_edges(final_one)
     halo_u[STEPS + 2].start()
-    pl.when(inner)(send_part)
-    for part in range(1, X - 1):
-        part_of_first(part)
+    for copy in by_x[1]:
+        copy.wait_recv()
+    over(H, R - H, final_one)
     depth(U.at[STEPS + 2], zu)
     over(H, R - H, final_two)
     halo_u[STEPS + 2].arrive()
@@ -558,7 +576,7 @@
     reduce_i.leave()
     for d, e in near:
         pl.when(is_near(d, e))(to_near(d, e).wait_send)
-    for copy in by_plane + by_x:
+    for copy in by_plane + sum(by_x, []):
         copy.wait_send()
 
 
@@ -593,7 +611,7 @@
     flat = (NX * R, D)
     padded = (R + 2 * H, NX + 2 * PAD, D)
     plain = (R, NX, D)
-    n_rs = X + Z * Y - 2
+    n_rs = Z * (X - 1) + Z * Y - 1
     n_near = 3 * (2 * -(-H // h) + 1)
     vmem, smem, anywhere = (
         pl.BlockSpec(memory_space=pltpu.VMEM),
@@ -616,7 +634,7 @@
             pltpu.VMEM((STEPS, *plain), f32),
             pltpu.VMEM(plain, f32),
             pltpu.VMEM(plain, f32),
-            pltpu.VMEM((2, max(X - 1, 1), q, NX, D), f32),
+            pltpu.VMEM((2, Z, X - 1, h, NX, D), f32),
             pltpu.VMEM((2, Z * Y - 1, h, c, D), f32),
             pltpu.VMEM((2, q, NX, D), f32),
             pltpu.VMEM((h + 2 * H, 3 * c, D), f32),

time: 79.3 us -> 73 us (0.921)
  the two profiles are of different devices: /device:TPU:1 before, /device:TPU:129 now
where the time goes in v4:
time: 73 us; the launch traced here: 72.8 us
  Pallas kernels  71.6 us (98%)
  between operations  1.29 us (2%)
    pallas_call x1, Pallas kernels, local(): pl.pallas_call(functools.partial(kernel, (X, Z, Y, boxes, NX, R)), out_sh...  70.4 us

profile of v4, /device:TPU:129, one launch (start us, length us, event | category | flops | bytes accessed | tf_op | source)
XLA Modules:
  0.0 72.8 jit_solution(2977159605952135525)
XLA Ops:
  1.3 70.4 %shard_map.112 = (f32[1024,128]{1,0:T(8,128)S(1)}, f32[1024,128]{1,0:T(8,128)S(1)}, f32[1024,128]{1,0:T(8,128)S(1)}) custom-call(s32[1]{0:T(128)S(6)} %copy.12.source_cell, f32[1,5]{1,0:T(1,128)} %wavelet.1, s32[1,128]{1,0:T(1,128)} %receiver_cell.1, f32[3,1,128]{2,1,0:T(1,128)} %bitcast.14, f32[1024,128]{1,0:T(8,128)} %bitcast.9, f32[1024,128]{1,0:T(8,128)} %bitcast.10, ...), custom_call_target="tpu_custom_call" | custom-call | tf_op jit(solution)/shard_map/pallas_call | solution.py:623
  71.7 1.2 %shard_map.113 = (f32[1024,128]{1,0:T(8,128)}, f32[1024,128]{1,0:T(8,128)}, f32[1024,128]{1,0:T(8,128)}) custom-call(f32[1024,128]{1,0:T(8,128)S(1)} %get-tuple-element.9.wave, f32[1024,128]{1,0:T(8,128)S(1)} %get-tuple-element.10.adjoint, f32[1024,128]{1,0:T(8,128)S(1)} %get-tuple-element.11.speed), custom_call_target="tpu_custom_call" | custom-call | tf_op jit(solution)/shard_map/pallas_call | solution.py:669

commit v5 on v4

--- a/solution.py
+++ b/solution.py
@@ -279,13 +279,13 @@
 
         return body
 
-    pl.semaphore_wait(barrier, count)
     loads[0].wait()
 
     def turn_wave(r):
         U[(1, *centre(r))] = turned(0, r)
 
     over(0, R, turn_wave)
+    pl.semaphore_wait(barrier, count)
     halo_u[1].start()
     loads[1].wait()
 

time: 73 us -> 72.6 us (level)
  no operation moved by 1% of the time
where the time goes in v5:
time: 72.6 us; the launch traced here: 72.4 us
  Pallas kernels  71.2 us (98%)
  between operations  1.29 us (2%)
    pallas_call x1, Pallas kernels, local(): pl.pallas_call(functools.partial(kernel, (X, Z, Y, boxes, NX, R)), out_sh...  70 us

profile of v5, /device:TPU:129, one launch (start us, length us, event | category | flops | bytes accessed | tf_op | source)
XLA Modules:
  0.0 72.4 jit_solution(768607609972328428)
XLA Ops:
  1.3 70.0 %shard_map.112 = (f32[1024,128]{1,0:T(8,128)S(1)}, f32[1024,128]{1,0:T(8,128)S(1)}, f32[1024,128]{1,0:T(8,128)S(1)}) custom-call(s32[1]{0:T(128)S(6)} %copy.12.source_cell, f32[1,5]{1,0:T(1,128)} %wavelet.1, s32[1,128]{1,0:T(1,128)} %receiver_cell.1, f32[3,1,128]{2,1,0:T(1,128)} %bitcast.14, f32[1024,128]{1,0:T(8,128)} %bitcast.9, f32[1024,128]{1,0:T(8,128)} %bitcast.10, ...), custom_call_target="tpu_custom_call" | custom-call | tf_op jit(solution)/shard_map/pallas_call | solution.py:623
  71.3 1.2 %shard_map.113 = (f32[1024,128]{1,0:T(8,128)}, f32[1024,128]{1,0:T(8,128)}, f32[1024,128]{1,0:T(8,128)}) custom-call(f32[1024,128]{1,0:T(8,128)S(1)} %get-tuple-element.9.wave, f32[1024,128]{1,0:T(8,128)S(1)} %get-tuple-element.10.adjoint, f32[1024,128]{1,0:T(8,128)S(1)} %get-tuple-element.11.speed), custom_call_target="tpu_custom_call" | custom-call | tf_op jit(solution)/shard_map/pallas_call | solution.py:669

commit v6 on v5

--- a/solution.py
+++ b/solution.py
@@ -424,19 +424,19 @@
     halo_u[2].arrive()
     over_edges(wave_row(2))
     halo_u[3].start()
+
+    def light(r):
+        one, two, three = (U[(t, *centre(r))] for t in range(1, 4))
+        I[r] = (one * one + two * two) + three * three
+
+    over(0, R, light)
+    reduce_i.start_x(1)
+    reduce_i.start_x(0)
     depth(W.at[2], zw)
     over(H, R - H, adjoint_row(2))
     depth(U.at[3], zu)
     over(H, R - H, wave_row(3))
     reduce_g.start_x(1)
-
-    def light(r):
-        one, two, three = (U[(t, *centre(r))] for t in range(1, 4))
-        I[r] = (one * one + two * two) + three * three
-
-    over(0, R, light)
-    reduce_i.start_x(1)
-    reduce_i.start_x(0)
     receive(3)
     halo_w[2].arrive()
     over_edges(adjoint_row(2))

time: 72.6 us -> 72.6 us (level)
  the two profiles are of different devices: /device:TPU:129 before, /device:TPU:1 now
where the time goes in v6:
time: 72.6 us; the launch traced here: 72.4 us
  Pallas kernels  71.1 us (98%)
  between operations  1.29 us (2%)
    pallas_call x1, Pallas kernels, local(): pl.pallas_call(functools.partial(kernel, (X, Z, Y, boxes, NX, R)), out_sh...  70 us

profile of v6, /device:TPU:1, one launch (start us, length us, event | category | flops | bytes accessed | tf_op | source)
XLA Modules:
  0.0 72.4 jit_solution(9684346249682222965)
XLA Ops:
  1.3 70.0 %shard_map.112 = (f32[1024,128]{1,0:T(8,128)S(1)}, f32[1024,128]{1,0:T(8,128)S(1)}, f32[1024,128]{1,0:T(8,128)S(1)}) custom-call(s32[1]{0:T(128)S(6)} %copy.12.source_cell, f32[1,5]{1,0:T(1,128)} %wavelet.1, s32[1,128]{1,0:T(1,128)} %receiver_cell.1, f32[3,1,128]{2,1,0:T(1,128)} %bitcast.14, f32[1024,128]{1,0:T(8,128)} %bitcast.9, f32[1024,128]{1,0:T(8,128)} %bitcast.10, ...), custom_call_target="tpu_custom_call" | custom-call | tf_op jit(solution)/shard_map/pallas_call | solution.py:623
  71.2 1.2 %shard_map.113 = (f32[1024,128]{1,0:T(8,128)}, f32[1024,128]{1,0:T(8,128)}, f32[1024,128]{1,0:T(8,128)}) custom-call(f32[1024,128]{1,0:T(8,128)S(1)} %get-tuple-element.9.wave, f32[1024,128]{1,0:T(8,128)S(1)} %get-tuple-element.10.adjoint, f32[1024,128]{1,0:T(8,128)S(1)} %get-tuple-element.11.speed), custom_call_target="tpu_custom_call" | custom-call | tf_op jit(solution)/shard_map/pallas_call | solution.py:669
